TPU v7x, 768 devices: a whole 4x8x12 slice. The times are simulated.
768 devices in a mesh: rep: 24 (over x, z_lo), fsdp: 32 (over y, z_hi, core).
Axes of the slice: x: 4, y: 8, z: 12 (z_hi: 2, z_lo: 6; z = z_hi * 6 + z_lo), core: 2. Of those that a mesh axis runs over, the one named last changes fastest.
Arguments:
- inputs: bfloat16 [147456, 4096], P(('rep', 'fsdp')), may hold values from -6 to 6
- key_grad: bfloat16 [147456, 512], P(('rep', 'fsdp')), may hold values from -16 to 16
- weights: float32 [24, 4096, 512], P('rep', 'fsdp'), may hold values from -6 to 6
- anchor: float32 [24, 4096, 512], P('rep', 'fsdp'), may hold values from -6 to 6
- adam_first: float32 [24, 4096, 512], P('rep', 'fsdp'), may hold values from -6 to 6
- adam_second: float32 [24, 4096, 512], P('rep', 'fsdp'), may hold values from 0.3 to 3
- outer_mom: float32 [24, 4096, 512], P('rep', 'fsdp'), may hold values from -6 to 6
- partner: int32 [32, 24], P('fsdp'), may hold values from 0 to 23, as said below
Outputs:
- keys: bfloat16 [147456, 512], P(('rep', 'fsdp'))
- new_anchor: float32 [24, 4096, 512], P('rep', 'fsdp')
- new_mom: float32 [24, 4096, 512], P('rep', 'fsdp')
- new_first: float32 [24, 4096, 512], P('rep', 'fsdp')
- new_second: float32 [24, 4096, 512], P('rep', 'fsdp')
Inputs may be any that keep to these rules, and one draw needn't show every extreme that they name: Each row partner[s] is a matching: partner[s, partner[s, r]] = r and partner[s, r] != r for every replica r.
All inputs are finite; a program needn't handle non-finite values.
Results may differ from a plain program's by a relative error of at most 0.019.
Values may be sent and summed in bfloat16 or wider, within the bound.
No kernel may reach another device: no remote copies, remote signals or barrier semaphores. Data moves between devices by JAX's collectives and lax.ppermute only.
A program may use at most 32 MiB of HBM per device.

v0:
```python
import jax
import jax.numpy as jnp
from jax import lax
from jax.sharding import PartitionSpec as P


def key_product(inputs, weights, scale):
    packed = weights[0].astype(jnp.bfloat16)
    gathered = lax.all_gather(packed, "fsdp", axis=0, tiled=True)
    key_sum = jnp.dot(inputs, gathered, preferred_element_type=jnp.float32)
    return (key_sum * scale).astype(jnp.bfloat16)


def grad_product(inputs, key_grad, scale):
    return lax.psum_scatter(
        (
            lax.dot_general(
                inputs, key_grad, (((0,), (0,)), ((), ())), preferred_element_type=jnp.float32
            )
            * scale
        ).astype(jnp.bfloat16),
        "fsdp",
        scatter_dimension=0,
        tiled=True,
    ).astype(jnp.float32)


def on_device(inputs, key_grad, weights, anchor, adam_first, adam_second, outer_mom, partner):
    scale = inputs.shape[1] ** (-0.5)
    rows = weights.shape[1]
    width = weights.shape[2]
    keys = key_product(inputs, weights, scale)
    grad = grad_product(inputs, key_grad, scale)
    weight = weights[0]
    first_new = 0.9 * adam_first[0] + 0.1 * grad
    second_new = 0.95 * adam_second[0] + 0.05 * grad * grad
    update = first_new / (1.0 - 0.9**8) / (jnp.sqrt(second_new / (1.0 - 0.95**8)) + 1e-08)
    inner = weight - 0.3 * (update + 0.1 * weight)
    delta = anchor[0] - inner
    matching = partner[0]
    replicas = lax.axis_size("rep")
    length = rows * width
    block = -(-length // (128 * replicas)) * 128
    stacked = jnp.stack([delta.reshape(length), outer_mom[0].reshape(length)])
    stacked = jnp.pad(stacked, ((0, 0), (0, replicas * block - length)))
    stacked = stacked.reshape(2, replicas, block)
    received = lax.all_to_all(
        stacked.astype(jnp.bfloat16), "rep", split_axis=1, concat_axis=1, tiled=True
    ).astype(stacked.dtype)
    averaged = 0.5 * (received + jnp.take(received, matching, axis=1))
    returned = lax.all_to_all(
        averaged.astype(jnp.bfloat16), "rep", split_axis=1, concat_axis=1, tiled=True
    ).astype(averaged.dtype)
    returned = returned.reshape(2, replicas * block)[:, :length].reshape(2, rows, width)
    mom_new = 0.5 * returned[1] + returned[0]
    step_value = 0.5 * mom_new + returned[0]
    anchor_new = anchor[0] - 0.7 * step_value
    return (keys, anchor_new[None], mom_new[None], first_new[None], second_new[None])


def solution(mesh):
    return jax.shard_map(
        on_device,
        mesh=mesh,
        in_specs=(
            P(("rep", "fsdp"), None),
            P(("rep", "fsdp"), None),
            P("rep", "fsdp", None),
            P("rep", "fsdp", None),
            P("rep", "fsdp", None),
            P("rep", "fsdp", None),
            P("rep", "fsdp", None),
            P("fsdp", None),
        ),
        out_specs=(
            P(("rep", "fsdp"), None),
            P("rep", "fsdp", None),
            P("rep", "fsdp", None),
            P("rep", "fsdp", None),
            P("rep", "fsdp", None),
        ),
        check_vma=False,
    )
```

profile of v0, /device:TPU:1, one launch (start us, length us, event | category | flops | bytes accessed | tf_op | source)
XLA Modules:
  0.0 332.8 jit_solution(2346534980045687941)
XLA Ops:
  7.2 0.0 copy-start
  7.2 0.0 reduce-scatter.2.cloned.1.call-start
  7.2 1.4 copy-done
  8.6 4.2 %multiply_convert_fusion = bf16[4096,512]{1,0:T(8,128)(2,1)} fusion(bf16[192,4096]{1,0:T(8,128)(2,1)S(1)} %copy-done, bf16[192,512]{1,0:T(8,128)(2,1)} %param.9), kind=kOutput, calls=%fused_computation.1 | convolution fusion | flops 809500672 | bytes 5963776 | tf_op jit(solution)/shard_map/dot_general | solution.py:17
  12.8 0.0 copy-start.4
  12.8 0.0 copy-start.6
  12.8 0.0 reduce-scatter.2.cloned.1.call-update
  12.8 0.0 all-gather.2.cloned.1.call-start
  12.9 0.8 copy-done.2
  13.7 0.7 bitcast_convert_fusion
  14.4 0.0 all-gather.2.cloned.1.call-update
  14.4 0.0 copy-done.5
  14.5 0.2 copy.14
  14.7 176.7 %reduce-scatter.2.cloned.1.call-done = bf16[128,512]{1,0:T(8,128)(2,1)} async-done(((bf16[4096,512]{1,0:T(8,128)(2,1)}), bf16[128,512]{1,0:T(8,128)(2,1)}) %reduce-scatter.2.cloned.1.call-update) | async-done | bytes 131088 | tf_op jit(solution)/shard_map/reduce_scatter | solution.py:15
  191.4 0.0 copy-done.1
  191.4 0.0 copy-done.3
  191.4 0.0 copy-done.4
  191.4 1.9 fusion.13
  193.3 0.2 copy.13
  193.5 1.3 fusion.5
  194.8 4.9 %all-to-all-start = ((bf16[2,24,2816]{2,0,1:T(2,128)(2,1)}), bf16[2,24,2816]{2,0,1:T(2,128)(2,1)S(1)}, u32[]{:S(2)}, u32[]{:S(2)}) async-start(bf16[2,24,2816]{2,0,1:T(2,128)(2,1)} %bitcast.4), calls=%async_computation.1 | async-start | bytes 540672 | tf_op jit(solution)/shard_map/all_to_all | solution.py:47
  199.7 0.0 copy-done.6
  199.8 11.6 %all-to-all-done = bf16[2,24,2816]{2,0,1:T(2,128)(2,1)S(1)} async-done(((bf16[2,24,2816]{2,0,1:T(2,128)(2,1)}), bf16[2,24,2816]{2,0,1:T(2,128)(2,1)S(1)}, u32[]{:S(2)}, u32[]{:S(2)}) %all-to-all-start) | async-done | bytes 270368 | tf_op jit(solution)/shard_map/all_to_all | solution.py:47
  211.4 0.2 convert_element_type.30
  211.6 1.1 gather_fusion
  212.8 0.5 fusion.4
  213.2 17.2 %all_to_all.10 = bf16[2,24,2816]{2,0,1:T(2,128)(2,1)S(1)} all-to-all(bf16[2,24,2816]{2,0,1:T(2,128)(2,1)S(1)} %fusion.4), channel_id=1, replica_groups=mesh['rep'=24,'fsdp'=32] {'rep'}, dimensions={1} | all-to-all | bytes 540672 | tf_op jit(solution)/shard_map/all_to_all | solution.py:51
  230.4 0.2 convert.13
  230.6 1.4 fusion.8
  232.1 0.9 multiply_subtract_fusion
  232.9 89.2 %all-gather.2.cloned.1.call-done = bf16[4096,512]{1,0:T(8,128)(2,1)} async-done(((bf16[128,512]{1,0:T(8,128)(2,1)}), bf16[4096,512]{1,0:T(8,128)(2,1)}) %all-gather.2.cloned.1.call-update) | async-done | bytes 4194320 | tf_op jit(solution)/shard_map/all_gather | solution.py:9
  322.1 3.8 %fusion = bf16[192,512]{1,0:T(8,128)(2,1)} fusion(bf16[192,4096]{1,0:T(8,128)(2,1)S(1)} %copy-done, bf16[4096,512]{1,0:T(8,128)(2,1)} %all-gather.2.cloned.1.call-done), kind=kOutput, calls=%fused_computation.3 | convolution fusion | flops 805502976 | bytes 5963776 | tf_op jit(solution)/shard_map/dot_general | solution.py:10
  (10 shorter events, 0.1 us)
Async XLA Ops:
  7.2 1.4 copy-start
  7.2 184.2 %reduce-scatter.2.cloned.1.call-start = ((), (), s32[]{:S(2)}) async-start(), calls=%async_computation.4 | async-start | bytes 4325376 | tf_op jit(solution)/shard_map/reduce_scatter | solution.py:15
  12.8 0.9 copy-start.2
  12.8 1.6 copy-start.5
  12.8 178.6 %copy-start.1 = (f32[1,128,512]{2,1,0:T(8,128)S(1)}, f32[1,128,512]{2,1,0:T(8,128)}, u32[]{:S(2)}) copy-start(f32[1,128,512]{2,1,0:T(8,128)} %param.11) | copy-start | bytes 786436
  12.8 178.6 %copy-start.3 = (f32[1,128,512]{2,1,0:T(8,128)S(1)}, f32[1,128,512]{2,1,0:T(8,128)}, u32[]{:S(2)}) copy-start(f32[1,128,512]{2,1,0:T(8,128)} %param.13) | copy-start | bytes 786436
  12.8 178.6 %copy-start.4 = (f32[1,128,512]{2,1,0:T(8,128)S(1)}, f32[1,128,512]{2,1,0:T(8,128)}, u32[]{:S(2)}) copy-start(f32[1,128,512]{2,1,0:T(8,128)} %param.12) | copy-start | bytes 786436
  12.8 186.9 %copy-start.6 = (s32[1,24]{1,0:T(1,128)S(1)}, s32[1,24]{1,0:T(1,128)}, u32[]{:S(2)}) copy-start(s32[1,24]{1,0:T(1,128)} %param.15) | copy-start | bytes 292
  12.8 309.3 %all-gather.2.cloned.1.call-start = ((), (), s32[]{:S(2)}) async-start(), calls=%async_computation.3 | async-start | bytes 4325376 | tf_op jit(solution)/shard_map/all_gather | solution.py:9
  194.8 16.6 %all-to-all-start = ((bf16[2,24,2816]{2,0,1:T(2,128)(2,1)}), bf16[2,24,2816]{2,0,1:T(2,128)(2,1)S(1)}, u32[]{:S(2)}, u32[]{:S(2)}) async-start(bf16[2,24,2816]{2,0,1:T(2,128)(2,1)} %bitcast.4), calls=%async_computation.1 | async-start | bytes 540672 | tf_op jit(solution)/shard_map/all_to_all | solution.py:47
Sparse Core Ops, SparseCore 0:
  13.4 177.9 reduce-scatter.1
  196.6 125.4 all-gather.1
where the time goes:
time: 333 us
  waiting for transfers between devices  278 us (83%)
  blocking collectives  17.2 us (5%)
  between operations  14.2 us (4%)
  matrix products  8.05 us (2%)
  other arithmetic  7.01 us (2%)
  starting transfers between devices  4.99 us (1%)
  local copies, waits for them, and re-layouts  3.85 us (1%)
    reduce_scatter x1, waiting for transfers between devices, grad_product(): lax.psum_scatter((lax.dot_general(inputs, key_grad, (((0,), (0,)), ((), (...  177 us
    all_gather x1, waiting for transfers between devices, key_product(): gathered = lax.all_gather(packed, 'fsdp', axis=0, tiled=True)  89.2 us
    all_to_all x1, blocking collectives, on_device(): lax.all_to_all(averaged.astype(jnp.bfloat16), 'rep', split_axis=1, concat...  17.2 us
    all_to_all x1, waiting for transfers between devices, on_device(): lax.all_to_all(stacked.astype(jnp.bfloat16), 'rep', split_axis=1, concat_...  11.6 us
  transfers between devices with their start and end apart: 3, of which 3 were waited for; matrix products, arithmetic and copies ran while one was open for 3% of the time, Pallas kernels for 0%

commit v1 on v0

v1 whole, which is shorter than its diff:
```python
import jax
import jax.numpy as jnp
from jax import lax
from jax.experimental import pallas as pl
from jax.experimental.pallas import tpu as pltpu
from jax.sharding import PartitionSpec as P

RING = 8
ORDER = (1, 3, 7, 5, 4, 2, 6, 0)
VMEM = pl.BlockSpec(memory_space=pltpu.VMEM)
HBM = pl.BlockSpec(memory_space=pl.ANY)
SMEM = pl.BlockSpec(memory_space=pltpu.SMEM)
PARAMS = pltpu.CompilerParams(vmem_limit_bytes=32 * 1024 * 1024)


def hop(move):
    pairs = []
    for y in range(RING):
        for z in range(2):
            for c in range(2):
                y2, z2, c2 = move(y, z, c)
                pairs.append(((y * 2 + z) * 2 + c, ((y2 % RING) * 2 + z2) * 2 + c2))
    return pairs


CORE = hop(lambda y, z, c: (y, z, 1 - c))
ZSWAP = hop(lambda y, z, c: (y, 1 - z, c))


def ring(step):
    return hop(lambda y, z, c: (y + step, z, c))


def send(value, pairs):
    return lax.ppermute(value, "fsdp", pairs)


def pick_kernel(table, x, k, own, other, sems):
    copies = [pltpu.make_async_copy(k, other.at[:, pl.ds(2048, 512)], sems.at[32])]
    for j in range(16):
        for half, target in ((0, own), (1, other)):
            start = pl.multiple_of(table[half * 16 + j] * 128, 128)
            copies.append(
                pltpu.make_async_copy(
                    x.at[:, pl.ds(start, 128)],
                    target.at[:, pl.ds(j * 128, 128)],
                    sems.at[half * 16 + j],
                )
            )
    for copy in copies:
        copy.start()
    for copy in copies:
        copy.wait()


def pick(inputs, key_grad, table):
    tokens = inputs.shape[0]
    return pl.pallas_call(
        pick_kernel,
        out_shape=(
            jax.ShapeDtypeStruct((tokens, 2048), jnp.bfloat16),
            jax.ShapeDtypeStruct((tokens, 2560), jnp.bfloat16),
        ),
        in_specs=[SMEM, HBM, HBM],
        out_specs=(HBM, HBM),
        scratch_shapes=[pltpu.SemaphoreType.DMA((33,))],
        compiler_params=PARAMS,
    )(table, inputs, key_grad)


def grad_kernel(scale, own, other, k, a, b, c1, c2, d2, d6, d0):
    right = jnp.concatenate([k[...], other[:, 2048:2560]], axis=0)
    places = (
        (a, 0), (a, 256), (b, 0), (b, 256), None, (d2, 0), (d6, 0), (d0, 0),
    )
    for p, place in enumerate(places):
        cols = slice(p * 256, p * 256 + 256)
        left = jnp.concatenate([own[:, cols], other[:, cols]], axis=0)
        part = scale * lax.dot_general(
            left, right, (((0,), (0,)), ((), ())), preferred_element_type=jnp.float32
        )
        if place is None:
            c1[...] = part[:128].astype(c1.dtype)
            c2[...] = part[128:].astype(c2.dtype)
        else:
            ref, row = place
            ref[row : row + 256, :] = part.astype(ref.dtype)


def grad_parts(own, other, key_grad, scale):
    bf = jnp.bfloat16
    shapes = ((512, bf), (512, bf), (128, bf), (128, bf), (256, bf), (256, bf), (256, jnp.float32))
    return pl.pallas_call(
        lambda *refs: grad_kernel(scale, *refs),
        out_shape=tuple(jax.ShapeDtypeStruct((rows, 512), kind) for rows, kind in shapes),
        in_specs=[VMEM] * 3,
        out_specs=(VMEM,) * 7,
        compiler_params=PARAMS,
        cost_estimate=pl.CostEstimate(
            flops=2 * 384 * 2048 * 512, bytes_accessed=5 << 20, transcendentals=0
        ),
    )(own, other, key_grad)


def key_kernel(scale, place, own, other, w, mine, theirs):
    y = place[0]
    total_mine = jnp.zeros(mine.shape, jnp.float32)
    total_theirs = jnp.zeros(theirs.shape, jnp.float32)
    for p, step in enumerate(ORDER):
        cols = slice(p * 256, p * 256 + 256)
        row = pl.multiple_of(lax.rem(y + step, RING) * 256, 256)
        block = w[pl.ds(row, 256), :]
        total_theirs += jnp.dot(other[:, cols], block, preferred_element_type=jnp.float32)
        total_mine += jnp.dot(own[:, cols], block, preferred_element_type=jnp.float32)
    mine[...] = scale * total_mine
    theirs[...] = (scale * total_theirs).astype(theirs.dtype)


def key_parts(place, own, other, w, scale):
    tokens = own.shape[0]
    return pl.pallas_call(
        lambda *refs: key_kernel(scale, *refs),
        out_shape=(
            jax.ShapeDtypeStruct((tokens, 512), jnp.float32),
            jax.ShapeDtypeStruct((tokens, 512), jnp.bfloat16),
        ),
        in_specs=[SMEM, VMEM, VMEM, VMEM],
        out_specs=(VMEM, VMEM),
        compiler_params=PARAMS,
        cost_estimate=pl.CostEstimate(
            flops=2 * 384 * 2048 * 512, bytes_accessed=5 << 20, transcendentals=0
        ),
    )(place, own, other, w)


def to_blocks(value, replicas):
    tiles = value.reshape(16, 8, 4, 128).transpose(0, 2, 1, 3).reshape(64, 8, 128)
    each = -(-64 // replicas)
    tiles = jnp.pad(tiles, ((0, replicas * each - 64), (0, 0), (0, 0)))
    return tiles.reshape(replicas, each * 8, 128)


def from_blocks(blocks):
    tiles = blocks.reshape(-1, 8, 128)[:64].reshape(16, 4, 8, 128)
    return tiles.transpose(0, 2, 1, 3).reshape(128, 512)


def average(value, matching):
    replicas = lax.axis_size("rep")
    blocks = to_blocks(value.astype(jnp.bfloat16), replicas)
    got = lax.all_to_all(blocks, "rep", split_axis=0, concat_axis=0, tiled=True)
    wide = got.astype(jnp.float32)
    mean = (0.5 * (wide + jnp.take(wide, matching, axis=0))).astype(jnp.bfloat16)
    back = lax.all_to_all(mean, "rep", split_axis=0, concat_axis=0, tiled=True)
    return from_blocks(back).astype(jnp.float32)


def on_device(inputs, key_grad, weights, anchor, adam_first, adam_second, outer_mom, partner):
    scale = inputs.shape[1] ** (-0.5)
    me = lax.axis_index("fsdp")
    core, zh, y = me % 2, (me // 2) % 2, me // 4
    groups = [[(r * 2 + z) * 2 + c for r in range(RING)] for z in range(2) for c in range(2)]
    matching = partner[0]
    weight = weights[0]

    steps = jnp.array(ORDER, jnp.int32)
    base = (lax.rem(y + steps, RING) * 4)[:, None] + jnp.stack([zh * 2, 2 - zh * 2])[None, :]
    base = base.reshape(16)
    table = jnp.concatenate([base + core, base + 1 - core]).astype(jnp.int32)
    own, away = pick(inputs, key_grad, table)
    other = send(away, CORE)

    packed = weight.astype(jnp.bfloat16)
    pair = jnp.concatenate([packed, send(packed, ZSWAP)], axis=0)
    gathered = lax.all_gather(pair, "fsdp", axis=0, tiled=True, axis_index_groups=groups)

    a, b, c1, c2, d2, d6, d0 = grad_parts(own, other, key_grad, scale)
    a, b = send(a, ring(1)), send(b, ring(-1))
    c1, c2 = send(c1, ring(2)), send(c2, ring(-2))
    f32 = jnp.float32
    m2 = d2.astype(f32) + a[256:].astype(f32) + jnp.pad(c1.astype(f32), ((0, 128), (0, 0)))
    m6 = d6.astype(f32) + b[256:].astype(f32) + jnp.pad(c2.astype(f32), ((128, 0), (0, 0)))
    e2 = send(m2.astype(jnp.bfloat16), ring(2))
    e6 = send(m6.astype(jnp.bfloat16), ring(-2))
    total = d0 + (a[:256].astype(f32) + b[:256].astype(f32)) + (e2.astype(f32) + e6.astype(f32))
    grad = total[:128] + send(total[128:].astype(jnp.bfloat16), ZSWAP).astype(f32)

    first_new = 0.9 * adam_first[0] + 0.1 * grad
    second_new = 0.95 * adam_second[0] + 0.05 * grad * grad
    update = first_new / (1.0 - 0.9**8) / (jnp.sqrt(second_new / (1.0 - 0.95**8)) + 1e-08)
    inner = weight - 0.3 * (update + 0.1 * weight)
    delta = anchor[0] - inner

    mom_avg = average(outer_mom[0], matching)
    delta_avg = average(delta, matching)
    mom_new = 0.5 * mom_avg + delta_avg
    anchor_new = anchor[0] - 0.7 * (0.5 * mom_new + delta_avg)

    place = jnp.reshape(y, (1,)).astype(jnp.int32)
    mine, theirs = key_parts(place, own, other, gathered, scale)
    keys = (mine + send(theirs, CORE).astype(f32)).astype(jnp.bfloat16)
    return (keys, anchor_new[None], mom_new[None], first_new[None], second_new[None])


def solution(mesh):
    shard = P("rep", "fsdp", None)
    flat = P(("rep", "fsdp"), None)
    return jax.shard_map(
        on_device,
        mesh=mesh,
        in_specs=(flat, flat, shard, shard, shard, shard, shard, P("fsdp", None)),
        out_specs=(flat, shard, shard, shard, shard),
        check_vma=False,
    )
```

time: 333 us -> 178 us (0.53)
  waiting for transfers between devices: 278 us -> 48.9 us
  starting transfers between devices: 4.99 us -> 76.3 us
  matrix products: 8.05 us -> 0 us
  Pallas kernels: 0 us -> 4.38 us
  other arithmetic: 7.01 us -> 11.3 us
  local copies, waits for them, and re-layouts: 3.85 us -> 7.29 us
    reduce_scatter x1 -> x0, waiting for transfers between devices: 177 us -> none  [grad_product(): lax.psum_scatter((lax.dot_general(inputs, key_grad, (((0,), (0,)), ((), (...]
    all_gather x1, waiting for transfers between devices: 89.2 us -> 0.02 us  [on_device(): lax.all_gather(pair, 'fsdp', axis=0, tiled=True, axis_index_groups=groups)]
    ppermute x0 -> x10, starting transfers between devices: none -> 53.3 us  [send(): return lax.ppermute(value, 'fsdp', pairs)]
    ppermute x0 -> x10, waiting for transfers between devices: none -> 28.4 us  [send(): return lax.ppermute(value, 'fsdp', pairs)]
    all_to_all x1 -> x3, starting transfers between devices: 4.91 us -> 22.9 us  [the longest x2 19.1 us: average(): got = lax.all_to_all(blocks, 'rep', split_axis=0, concat_axis=0, tiled=True)]
    all_to_all x1 -> x3, waiting for transfers between devices: 11.6 us -> 20.5 us  [the longest x1 10.6 us: average(): back = lax.all_to_all(mean, 'rep', split_axis=0, concat_axis=0, tiled=True)]
    dot_general x2 -> x0, matrix products: 8.05 us -> none  [the longest x1 4.2 us: grad_product(): lax.dot_general(inputs, key_grad, (((0,), (0,)), ((), ())), preferred_ele...]
    pallas_call x0 -> x3, Pallas kernels: none -> 4.38 us  [the longest x1 1.94 us: grad_parts(): pl.pallas_call(lambda *refs: grad_kernel(scale, *refs), out_shape=tuple((...]
  transfers between devices with their start and end apart: 3 -> 14, of which waited for: 3 -> 7; matrix products, arithmetic and copies ran while one was open for 3% -> 7% of each run, Pallas kernels for 0% -> 1%
where the time goes in v1:
time: 178 us; the launch traced here: 177 us
  starting transfers between devices  76.3 us (43%)
  waiting for transfers between devices  48.9 us (27%)
  between operations  14.4 us (8%)
  blocking collectives  14.2 us (8%)
  other arithmetic  11.3 us (6%)
  local copies, waits for them, and re-layouts  7.29 us (4%)
  Pallas kernels  4.38 us (2%)
    ppermute x10, starting transfers between devices, send(): return lax.ppermute(value, 'fsdp', pairs)  53.3 us
    ppermute x10, waiting for transfers between devices, send(): return lax.ppermute(value, 'fsdp', pairs)  28.4 us
    all_to_all x2, starting transfers between devices, average(): got = lax.all_to_all(blocks, 'rep', split_axis=0, concat_axis=0, tiled=True)  19.1 us
    all_to_all x1, blocking collectives, average(): back = lax.all_to_all(mean, 'rep', split_axis=0, concat_axis=0, tiled=True)  14.2 us
    all_to_all x1, waiting for transfers between devices, average(): back = lax.all_to_all(mean, 'rep', split_axis=0, concat_axis=0, tiled=True)  10.6 us
    all_to_all x2, waiting for transfers between devices, average(): got = lax.all_to_all(blocks, 'rep', split_axis=0, concat_axis=0, tiled=True)  9.94 us
    unnamed x16, local copies, waits for them, and re-layouts  4.6 us
    all_to_all x1, starting transfers between devices, average(): back = lax.all_to_all(mean, 'rep', split_axis=0, concat_axis=0, tiled=True)  3.83 us
  transfers between devices with their start and end apart: 14, of which 7 were waited for; matrix products, arithmetic and copies ran while one was open for 7% of the time, Pallas kernels for 1%

profile of v1, /device:TPU:1, one launch (start us, length us, event | category | flops | bytes accessed | tf_op | source)
XLA Modules:
  0.0 176.7 jit_solution(13100808473535348839)
XLA Ops:
  8.3 1.4 copy-done.1
  9.7 0.9 copy-done.2
  10.6 1.5 shard_map.128
  12.1 12.4 %collective-permute-start = (bf16[192,2560]{1,0:T(8,128)(2,1)S(1)}, bf16[192,2560]{1,0:T(8,128)(2,1)S(1)}, u32[]{:S(2)}, u32[]{:S(2)}) collective-permute-start(bf16[192,2560]{1,0:T(8,128)(2,1)S(1)} %get-tuple-element.18), channel_id=1, source_target_pairs={{0,1},{1,0},{2,3},{3,2},{4,5},{5,4},{6,7},{7,6},{8,9},{9,8},{10,11... | collective-permute-start | bytes 2949128 | tf_op jit(solution)/shard_map/ppermute | solution.py:35
  24.6 1.0 bitcast_convert_fusion
  25.5 5.8 %collective-permute-start.1 = (bf16[128,512]{1,0:T(8,128)(2,1)S(1)}, bf16[128,512]{1,0:T(8,128)(2,1)S(1)}, u32[]{:S(2)}, u32[]{:S(2)}) collective-permute-start(bf16[128,512]{1,0:T(8,128)(2,1)S(1)} %bitcast_convert_fusion), channel_id=1, source_target_pairs={{0,2},{1,3},{2,0},{3,1},{4,6},{5,7},{6,4},{7,5},{8,10},{9,11},{10,... | collective-permute-start | bytes 393224 | tf_op jit(solution)/shard_map/ppermute | solution.py:35
  31.4 1.9 %shard_map.130 = (bf16[512,512]{1,0:T(8,128)(2,1)S(1)}, bf16[512,512]{1,0:T(8,128)(2,1)}, bf16[128,512]{1,0:T(8,128)(2,1)S(1)}, bf16[128,512]{1,0:T(8,128)(2,1)S...) custom-call(bf16[192,2048]{1,0:T(8,128)(2,1)S(1)} %get-tuple-element.17.refs_1_.refs_0_, ...), custom_call_target="tpu_custom_call" | custom-call | flops 805306368 | bytes 5242880 | tf_op jit(solution)/shard_map/pallas_call | solution.py:93
  34.0 5.1 %collective-permute-start.4 = (bf16[512,512]{1,0:T(8,128)(2,1)}, bf16[512,512]{1,0:T(8,128)(2,1)}, u32[]{:S(2)}, u32[]{:S(2)}) collective-permute-start(bf16[512,512]{1,0:T(8,128)(2,1)} %get-tuple-element.23), channel_id=1, source_target_pairs={{0,28},{1,29},{2,30},{3,31},{4,0},{5,1},{6,2},{7,3},{8,4},{9,5},{1... | collective-permute-start | bytes 1572872 | tf_op jit(solution)/shard_map/ppermute | solution.py:35
  39.8 1.9 %collective-permute-start.3 = (bf16[512,512]{1,0:T(8,128)(2,1)S(1)}, bf16[512,512]{1,0:T(8,128)(2,1)S(1)}, u32[]{:S(2)}, u32[]{:S(2)}) collective-permute-start(bf16[512,512]{1,0:T(8,128)(2,1)S(1)} %get-tuple-element.22), channel_id=1, source_target_pairs={{0,4},{1,5},{2,6},{3,7},{4,8},{5,9},{6,10},{7,11},{8,12},{9,13},{1... | collective-permute-start | bytes 1572872 | tf_op jit(solution)/shard_map/ppermute | solution.py:35
  41.8 4.1 %collective-permute-start.7 = (bf16[128,512]{1,0:T(8,128)(2,1)}, bf16[128,512]{1,0:T(8,128)(2,1)S(1)}, u32[]{:S(2)}, u32[]{:S(2)}) collective-permute-start(bf16[128,512]{1,0:T(8,128)(2,1)} %copy-done.3), channel_id=1, source_target_pairs={{0,24},{1,25},{2,26},{3,27},{4,28},{5,29},{6,30},{7,31},{8,0},{9,1... | collective-permute-start | bytes 393224 | tf_op jit(solution)/shard_map/ppermute | solution.py:35
  45.9 2.0 %collective-permute-start.5 = (bf16[128,512]{1,0:T(8,128)(2,1)S(1)}, bf16[128,512]{1,0:T(8,128)(2,1)S(1)}, u32[]{:S(2)}, u32[]{:S(2)}) collective-permute-start(bf16[128,512]{1,0:T(8,128)(2,1)S(1)} %get-tuple-element.25), channel_id=1, source_target_pairs={{0,8},{1,9},{2,10},{3,11},{4,12},{5,13},{6,14},{7,15},{8,16},{9,17... | collective-permute-start | bytes 393224 | tf_op jit(solution)/shard_map/ppermute | solution.py:35
  48.0 8.1 %collective-permute-done.7 = bf16[128,512]{1,0:T(8,128)(2,1)S(1)} collective-permute-done((bf16[128,512]{1,0:T(8,128)(2,1)}, bf16[128,512]{1,0:T(8,128)(2,1)S(1)}, u32[]{:S(2)}, u32[]{:S(2)}) %collective-permute-start.7) | collective-permute-done | bytes 131104 | tf_op jit(solution)/shard_map/ppermute | solution.py:35
  56.0 1.7 add_convert_fusion
  57.8 6.1 %collective-permute-start.8 = (bf16[256,512]{1,0:T(8,128)(2,1)}, bf16[256,512]{1,0:T(8,128)(2,1)}, u32[]{:S(2)}, u32[]{:S(2)}) collective-permute-start(bf16[256,512]{1,0:T(8,128)(2,1)} %add_convert_fusion), channel_id=1, source_target_pairs={{0,24},{1,25},{2,26},{3,27},{4,28},{5,29},{6,30},{7,31},{8,0},{9,1... | collective-permute-start | bytes 786440 | tf_op jit(solution)/shard_map/ppermute | solution.py:35
  64.0 2.1 %collective-permute-start.6 = (bf16[256,512]{1,0:T(8,128)(2,1)S(1)}, bf16[256,512]{1,0:T(8,128)(2,1)}, u32[]{:S(2)}, u32[]{:S(2)}) collective-permute-start(bf16[256,512]{1,0:T(8,128)(2,1)S(1)} %add_convert_fusion.1), channel_id=1, source_target_pairs={{0,8},{1,9},{2,10},{3,11},{4,12},{5,13},{6,14},{7,15},{8,16},{9,17... | collective-permute-start | bytes 786440 | tf_op jit(solution)/shard_map/ppermute | solution.py:35
  66.1 1.0 convert_element_type.117
  67.7 8.8 %all-to-all-start = ((bf16[24,24,128]{2,1,0:T(8,128)(2,1)}), bf16[24,24,128]{2,1,0:T(8,128)(2,1)S(1)}, u32[]{:S(2)}, u32[]{:S(2)}) async-start(bf16[24,24,128]{2,1,0:T(8,128)(2,1)} %bitcast.7), calls=%async_computation | async-start | bytes 294912 | tf_op jit(solution)/shard_map/all_to_all | solution.py:151
  76.5 3.8 %collective-permute-done.8 = bf16[256,512]{1,0:T(8,128)(2,1)} collective-permute-done((bf16[256,512]{1,0:T(8,128)(2,1)}, bf16[256,512]{1,0:T(8,128)(2,1)}, u32[]{:S(2)}, u32[]{:S(2)}) %collective-permute-start.8) | collective-permute-done | bytes 262176 | tf_op jit(solution)/shard_map/ppermute | solution.py:35
  80.4 5.5 %collective-permute-done.6 = bf16[256,512]{1,0:T(8,128)(2,1)} collective-permute-done((bf16[256,512]{1,0:T(8,128)(2,1)S(1)}, bf16[256,512]{1,0:T(8,128)(2,1)}, u32[]{:S(2)}, u32[]{:S(2)}) %collective-permute-start.6) | collective-permute-done | bytes 262176 | tf_op jit(solution)/shard_map/ppermute | solution.py:35
  85.9 1.4 add_add_fusion
  87.3 1.9 %collective-permute-start.9 = (bf16[128,512]{1,0:T(8,128)(2,1)S(1)}, bf16[128,512]{1,0:T(8,128)(2,1)S(1)}, u32[]{:S(2)}, u32[]{:S(2)}) collective-permute-start(bf16[128,512]{1,0:T(8,128)(2,1)S(1)} %slice.64), channel_id=1, source_target_pairs={{0,2},{1,3},{2,0},{3,1},{4,6},{5,7},{6,4},{7,5},{8,10},{9,11},{10,... | collective-permute-start | bytes 393224 | tf_op jit(solution)/shard_map/ppermute | solution.py:35
  89.2 10.8 %collective-permute-done.9 = bf16[128,512]{1,0:T(8,128)(2,1)S(1)} collective-permute-done((bf16[128,512]{1,0:T(8,128)(2,1)S(1)}, bf16[128,512]{1,0:T(8,128)(2,1)S(1)}, u32[]{:S(2)}, u32[]{:S(2)}) %collective-permute-start.9) | collective-permute-done | bytes 131104 | tf_op jit(solution)/shard_map/ppermute | solution.py:35
  100.0 2.0 %fusion.14 = (f32[1,128,512]{2,1,0:T(8,128)}, bf16[128,512]{1,0:T(8,128)(2,1)S(1)}, f32[1,128,512]{2,1,0:T(8,128)}) fusion(bf16[128,512]{1,0:T(8,128)(2,1)S(1)} %collective-permute-done.9, f32[256,512]{1,0:T(8,128)S(1)} %add_add_fusion, f32[1,128,512]{2,1,0:T(8,128)} %param.16, f32[1,128,512]{2,1,0:T(8,128)} %param.15, f32[1,128,512]{2,1,0:T(8,128)S(1)} %copy-done.4, ...), kind=kLoop, calls=%fused_computation.43 | loop fusion | flops 1245184 | bytes 2097152 | tf_op jit(solution)/shard_map/broadcast_in_dim | solution.py:202
  102.7 10.3 %all-to-all-start.2 = ((bf16[24,24,128]{2,1,0:T(8,128)(2,1)}), bf16[24,24,128]{2,1,0:T(8,128)(2,1)S(1)}, u32[]{:S(2)}, u32[]{:S(2)}) async-start(bf16[24,24,128]{2,1,0:T(8,128)(2,1)} %bitcast.19), calls=%async_computation.2 | async-start | bytes 294912 | tf_op jit(solution)/shard_map/all_to_all | solution.py:151
  113.7 9.9 %all-to-all-done.2 = bf16[24,24,128]{2,1,0:T(8,128)(2,1)S(1)} async-done(((bf16[24,24,128]{2,1,0:T(8,128)(2,1)}), bf16[24,24,128]{2,1,0:T(8,128)(2,1)S(1)}, u32[]{:S(2)}, u32[]{:S(2)}) %all-to-all-start.2) | async-done | bytes 147488 | tf_op jit(solution)/shard_map/all_to_all | solution.py:151
  125.0 14.2 %all_to_all.20 = bf16[24,24,128]{2,1,0:T(8,128)(2,1)S(1)} all-to-all(bf16[24,24,128]{2,1,0:T(8,128)(2,1)S(1)} %get-tuple-element.36), channel_id=1, replica_groups=mesh['rep'=24,'fsdp'=32] {'rep'}, dimensions={0} | all-to-all | bytes 294912 | tf_op jit(solution)/shard_map/all_to_all | solution.py:154
  139.2 3.8 %all-to-all-start.1 = ((bf16[24,24,128]{2,1,0:T(8,128)(2,1)}), bf16[24,24,128]{2,1,0:T(8,128)(2,1)S(1)}, u32[]{:S(2)}, u32[]{:S(2)}) async-start(bf16[24,24,128]{2,1,0:T(8,128)(2,1)} %get-tuple-element.35), calls=%async_computation.1 | async-start | bytes 294912 | tf_op jit(solution)/shard_map/all_to_all | solution.py:154
  143.1 10.6 %all-to-all-done.1 = bf16[24,24,128]{2,1,0:T(8,128)(2,1)S(1)} async-done(((bf16[24,24,128]{2,1,0:T(8,128)(2,1)}), bf16[24,24,128]{2,1,0:T(8,128)(2,1)S(1)}, u32[]{:S(2)}, u32[]{:S(2)}) %all-to-all-start.1) | async-done | bytes 147488 | tf_op jit(solution)/shard_map/all_to_all | solution.py:154
  153.7 1.6 copy-done
  155.3 1.0 shard_map.129
  156.3 11.8 %collective-permute-start.2 = (bf16[192,512]{1,0:T(8,128)(2,1)S(1)}, bf16[192,512]{1,0:T(8,128)(2,1)S(1)}, u32[]{:S(2)}, u32[]{:S(2)}) collective-permute-start(bf16[192,512]{1,0:T(8,128)(2,1)S(1)} %get-tuple-element.20), channel_id=1, source_target_pairs={{0,1},{1,0},{2,3},{3,2},{4,5},{5,4},{6,7},{7,6},{8,9},{9,8},{10,11... | collective-permute-start | bytes 589832 | tf_op jit(solution)/shard_map/ppermute | solution.py:35
  168.0 0.9 fusion.6
  (45 shorter events, 7.0 us)
Async XLA Ops:
  7.2 146.5 %all-gather.2.cloned.1.call-start = ((), (), s32[]{:S(2)}) async-start(), calls=%async_computation.4 | async-start | bytes 2359296 | tf_op jit(solution)/shard_map/all_gather | solution.py:175
  8.3 1.4 copy-start.1
  9.7 0.9 copy-start.2
  12.1 19.3 %collective-permute-start = (bf16[192,2560]{1,0:T(8,128)(2,1)S(1)}, bf16[192,2560]{1,0:T(8,128)(2,1)S(1)}, u32[]{:S(2)}, u32[]{:S(2)}) collective-permute-start(bf16[192,2560]{1,0:T(8,128)(2,1)S(1)} %get-tuple-element.18), channel_id=1, source_target_pairs={{0,1},{1,0},{2,3},{3,2},{4,5},{5,4},{6,7},{7,6},{8,9},{9,8},{10,11... | collective-permute-start | bytes 2949128 | tf_op jit(solution)/shard_map/ppermute | solution.py:35
  25.5 13.6 %collective-permute-start.1 = (bf16[128,512]{1,0:T(8,128)(2,1)S(1)}, bf16[128,512]{1,0:T(8,128)(2,1)S(1)}, u32[]{:S(2)}, u32[]{:S(2)}) collective-permute-start(bf16[128,512]{1,0:T(8,128)(2,1)S(1)} %bitcast_convert_fusion), channel_id=1, source_target_pairs={{0,2},{1,3},{2,0},{3,1},{4,6},{5,7},{6,4},{7,5},{8,10},{9,11},{10,... | collective-permute-start | bytes 393224 | tf_op jit(solution)/shard_map/ppermute | solution.py:35
  33.3 0.7 copy-start.3
  34.0 22.0 %collective-permute-start.4 = (bf16[512,512]{1,0:T(8,128)(2,1)}, bf16[512,512]{1,0:T(8,128)(2,1)}, u32[]{:S(2)}, u32[]{:S(2)}) collective-permute-start(bf16[512,512]{1,0:T(8,128)(2,1)} %get-tuple-element.23), channel_id=1, source_target_pairs={{0,28},{1,29},{2,30},{3,31},{4,0},{5,1},{6,2},{7,3},{8,4},{9,5},{1... | collective-permute-start | bytes 1572872 | tf_op jit(solution)/shard_map/ppermute | solution.py:35
  39.8 24.0 %collective-permute-start.3 = (bf16[512,512]{1,0:T(8,128)(2,1)S(1)}, bf16[512,512]{1,0:T(8,128)(2,1)S(1)}, u32[]{:S(2)}, u32[]{:S(2)}) collective-permute-start(bf16[512,512]{1,0:T(8,128)(2,1)S(1)} %get-tuple-element.22), channel_id=1, source_target_pairs={{0,4},{1,5},{2,6},{3,7},{4,8},{5,9},{6,10},{7,11},{8,12},{9,13},{1... | collective-permute-start | bytes 1572872 | tf_op jit(solution)/shard_map/ppermute | solution.py:35
  41.8 14.3 %collective-permute-start.7 = (bf16[128,512]{1,0:T(8,128)(2,1)}, bf16[128,512]{1,0:T(8,128)(2,1)S(1)}, u32[]{:S(2)}, u32[]{:S(2)}) collective-permute-start(bf16[128,512]{1,0:T(8,128)(2,1)} %copy-done.3), channel_id=1, source_target_pairs={{0,24},{1,25},{2,26},{3,27},{4,28},{5,29},{6,30},{7,31},{8,0},{9,1... | collective-permute-start | bytes 393224 | tf_op jit(solution)/shard_map/ppermute | solution.py:35
  45.9 17.9 %collective-permute-start.5 = (bf16[128,512]{1,0:T(8,128)(2,1)S(1)}, bf16[128,512]{1,0:T(8,128)(2,1)S(1)}, u32[]{:S(2)}, u32[]{:S(2)}) collective-permute-start(bf16[128,512]{1,0:T(8,128)(2,1)S(1)} %get-tuple-element.25), channel_id=1, source_target_pairs={{0,8},{1,9},{2,10},{3,11},{4,12},{5,13},{6,14},{7,15},{8,16},{9,17... | collective-permute-start | bytes 393224 | tf_op jit(solution)/shard_map/ppermute | solution.py:35
  57.8 22.6 %collective-permute-start.8 = (bf16[256,512]{1,0:T(8,128)(2,1)}, bf16[256,512]{1,0:T(8,128)(2,1)}, u32[]{:S(2)}, u32[]{:S(2)}) collective-permute-start(bf16[256,512]{1,0:T(8,128)(2,1)} %add_convert_fusion), channel_id=1, source_target_pairs={{0,24},{1,25},{2,26},{3,27},{4,28},{5,29},{6,30},{7,31},{8,0},{9,1... | collective-permute-start | bytes 786440 | tf_op jit(solution)/shard_map/ppermute | solution.py:35
  63.9 3.8 %copy-start.6 = (bf16[512,512]{1,0:T(8,128)(2,1)}, bf16[512,512]{1,0:T(8,128)(2,1)S(1)}, u32[]{:S(2)}) copy-start(bf16[512,512]{1,0:T(8,128)(2,1)S(1)} %collective-permute-done.3) | copy-start | bytes 1572868
  63.9 36.1 %copy-start.4 = (f32[1,128,512]{2,1,0:T(8,128)S(1)}, f32[1,128,512]{2,1,0:T(8,128)}, u32[]{:S(2)}) copy-start(f32[1,128,512]{2,1,0:T(8,128)} %param.13) | copy-start | bytes 786436
  63.9 36.1 %copy-start.5 = (f32[1,128,512]{2,1,0:T(8,128)S(1)}, f32[1,128,512]{2,1,0:T(8,128)}, u32[]{:S(2)}) copy-start(f32[1,128,512]{2,1,0:T(8,128)} %param.14) | copy-start | bytes 786436
  64.0 21.9 %collective-permute-start.6 = (bf16[256,512]{1,0:T(8,128)(2,1)S(1)}, bf16[256,512]{1,0:T(8,128)(2,1)}, u32[]{:S(2)}, u32[]{:S(2)}) collective-permute-start(bf16[256,512]{1,0:T(8,128)(2,1)S(1)} %add_convert_fusion.1), channel_id=1, source_target_pairs={{0,8},{1,9},{2,10},{3,11},{4,12},{5,13},{6,14},{7,15},{8,16},{9,17... | collective-permute-start | bytes 786440 | tf_op jit(solution)/shard_map/ppermute | solution.py:35
  67.7 35.0 %all-to-all-start = ((bf16[24,24,128]{2,1,0:T(8,128)(2,1)}), bf16[24,24,128]{2,1,0:T(8,128)(2,1)S(1)}, u32[]{:S(2)}, u32[]{:S(2)}) async-start(bf16[24,24,128]{2,1,0:T(8,128)(2,1)} %bitcast.7), calls=%async_computation | async-start | bytes 294912 | tf_op jit(solution)/shard_map/all_to_all | solution.py:151
  85.9 27.1 %copy-start.7 = (s32[1,24]{1,0:T(1,128)S(1)}, s32[1,24]{1,0:T(1,128)}, u32[]{:S(2)}) copy-start(s32[1,24]{1,0:T(1,128)} %param.18) | copy-start | bytes 292
  87.3 12.7 %collective-permute-start.9 = (bf16[128,512]{1,0:T(8,128)(2,1)S(1)}, bf16[128,512]{1,0:T(8,128)(2,1)S(1)}, u32[]{:S(2)}, u32[]{:S(2)}) collective-permute-start(bf16[128,512]{1,0:T(8,128)(2,1)S(1)} %slice.64), channel_id=1, source_target_pairs={{0,2},{1,3},{2,0},{3,1},{4,6},{5,7},{6,4},{7,5},{8,10},{9,11},{10,... | collective-permute-start | bytes 393224 | tf_op jit(solution)/shard_map/ppermute | solution.py:35
  102.7 20.9 %all-to-all-start.2 = ((bf16[24,24,128]{2,1,0:T(8,128)(2,1)}), bf16[24,24,128]{2,1,0:T(8,128)(2,1)S(1)}, u32[]{:S(2)}, u32[]{:S(2)}) async-start(bf16[24,24,128]{2,1,0:T(8,128)(2,1)} %bitcast.19), calls=%async_computation.2 | async-start | bytes 294912 | tf_op jit(solution)/shard_map/all_to_all | solution.py:151
  139.2 14.4 %all-to-all-start.1 = ((bf16[24,24,128]{2,1,0:T(8,128)(2,1)}), bf16[24,24,128]{2,1,0:T(8,128)(2,1)S(1)}, u32[]{:S(2)}, u32[]{:S(2)}) async-start(bf16[24,24,128]{2,1,0:T(8,128)(2,1)} %get-tuple-element.35), calls=%async_computation.1 | async-start | bytes 294912 | tf_op jit(solution)/shard_map/all_to_all | solution.py:154
  153.7 1.6 copy-start
  156.3 12.8 %collective-permute-start.2 = (bf16[192,512]{1,0:T(8,128)(2,1)S(1)}, bf16[192,512]{1,0:T(8,128)(2,1)S(1)}, u32[]{:S(2)}, u32[]{:S(2)}) collective-permute-start(bf16[192,512]{1,0:T(8,128)(2,1)S(1)} %get-tuple-element.20), channel_id=1, source_target_pairs={{0,1},{1,0},{2,3},{3,2},{4,5},{5,4},{6,7},{7,6},{8,9},{9,8},{10,11... | collective-permute-start | bytes 589832 | tf_op jit(solution)/shard_map/ppermute | solution.py:35
Sparse Core Ops, SparseCore 0:
  40.0 56.1 all-gather.1

commit v2 on v0

v2 whole, which is shorter than its diff:
```python
import jax
import jax.numpy as jnp
from jax import lax
from jax.experimental import pallas as pl
from jax.experimental.pallas import tpu as pltpu
from jax.sharding import PartitionSpec as P

RING = 8
ORDER = (1, 3, 7, 5, 4, 2, 6, 0)
VMEM = pl.BlockSpec(memory_space=pltpu.VMEM)
ANY = pl.BlockSpec(memory_space=pl.ANY)
HBM = pl.BlockSpec(memory_space=pltpu.HBM)
SMEM = pl.BlockSpec(memory_space=pltpu.SMEM)
PARAMS = pltpu.CompilerParams(vmem_limit_bytes=10 * 1024 * 1024)
BF16 = jnp.bfloat16
F32 = jnp.float32


def hop(move):
    pairs = []
    for y in range(RING):
        for z in range(2):
            for c in range(2):
                y2, z2, c2 = move(y, z, c)
                pairs.append(((y * 2 + z) * 2 + c, ((y2 % RING) * 2 + z2) * 2 + c2))
    return pairs


CORE = hop(lambda y, z, c: (y, z, 1 - c))
ZSWAP = hop(lambda y, z, c: (y, 1 - z, c))


def ring(step):
    return hop(lambda y, z, c: (y + (1 - 2 * c) * step, z, c))


def send(value, pairs):
    return lax.ppermute(value, "fsdp", pairs)


def place():
    me = lax.axis_index("fsdp")
    return lax.rem(me, 2), lax.rem(lax.div(me, 2), 2), lax.div(me, 4)


def pick_kernel(away, x, *refs):
    core, zh, y = place()
    if away:
        k, out, sems = refs
        core = 1 - core
        copies = [pltpu.make_async_copy(k, out.at[:, pl.ds(2048, 512)], sems.at[16])]
    else:
        out, sems = refs
        copies = []
    for p, step in enumerate(ORDER):
        chunk = lax.rem(y + RING + (1 - 2 * core) * step, RING)
        for half in range(2):
            z = zh if half == 0 else 1 - zh
            start = pl.multiple_of((chunk * 4 + z * 2 + core) * 128, 128)
            j = 2 * p + half
            copies.append(
                pltpu.make_async_copy(
                    x.at[:, pl.ds(start, 128)], out.at[:, pl.ds(j * 128, 128)], sems.at[j]
                )
            )
    for copy in copies:
        copy.start()
    for copy in copies:
        copy.wait()


def pick(away, *operands):
    width = 2560 if away else 2048
    return pl.pallas_call(
        lambda *refs: pick_kernel(away, *refs),
        out_shape=jax.ShapeDtypeStruct((operands[0].shape[0], width), BF16),
        in_specs=[HBM] * len(operands),
        out_specs=ANY,
        scratch_shapes=[pltpu.SemaphoreType.DMA((17,))],
        compiler_params=PARAMS,
    )(*operands)


def call(kernel, shapes, specs, *operands, flops=0):
    return pl.pallas_call(
        kernel,
        out_shape=tuple(jax.ShapeDtypeStruct(shape, kind) for shape, kind in shapes),
        in_specs=specs,
        out_specs=(VMEM,) * len(shapes),
        compiler_params=PARAMS,
        cost_estimate=pl.CostEstimate(flops=flops, bytes_accessed=1 << 20, transcendentals=0),
    )(*operands)


def grad_kernel(scale, own, other, k, a, b, c4, d2, d6, d0):
    right = jnp.concatenate([k[...], other[:, 2048:2560]], axis=0)
    targets = ((a, 0), (a, 256), (b, 0), (b, 256), (c4, 0), (d2, 0), (d6, 0), (d0, 0))
    for p, (ref, row) in enumerate(targets):
        cols = slice(p * 256, p * 256 + 256)
        left = jnp.concatenate([own[:, cols], other[:, cols]], axis=0)
        part = scale * lax.dot_general(
            left, right, (((0,), (0,)), ((), ())), preferred_element_type=F32
        )
        ref[row : row + 256, :] = part.astype(ref.dtype)


def relay_kernel(d2, d6, a, b, c4, m2, m6):
    m2[...] = (d2[...] + a[256:, :].astype(F32) + c4[...].astype(F32)).astype(BF16)
    m6[...] = (d6[...] + b[256:, :].astype(F32)).astype(BF16)


def sum_of(d0, a, b, e2, e6, rows):
    near = a[rows, :].astype(F32) + b[rows, :].astype(F32)
    return d0[rows, :] + near + (e2[rows, :].astype(F32) + e6[rows, :].astype(F32))


def far_kernel(d0, a, b, e2, e6, out):
    out[...] = sum_of(d0, a, b, e2, e6, slice(128, 256)).astype(BF16)


def adam_kernel(d0, a, b, e2, e6, far, weight, anchor, first, second, mom, first_out, second_out, blocks):
    blocks[...] = jnp.zeros(blocks.shape, BF16)
    tiles, moms = [], []
    for r in range(8):
        rows = slice(16 * r, 16 * r + 16)
        grad = sum_of(d0, a, b, e2, e6, rows) + far[rows, :].astype(F32)
        first_new = 0.9 * first[0, rows, :] + 0.1 * grad
        second_new = 0.95 * second[0, rows, :] + 0.05 * grad * grad
        first_out[0, rows, :] = first_new
        second_out[0, rows, :] = second_new
        update = first_new / (1.0 - 0.9**8) / (jnp.sqrt(second_new / (1.0 - 0.95**8)) + 1e-08)
        w = weight[0, rows, :]
        delta = anchor[0, rows, :] - (w - 0.3 * (update + 0.1 * w))
        m = mom[0, rows, :]
        for s in range(2):
            for c in range(4):
                tiles.append(delta[8 * s : 8 * s + 8, 128 * c : 128 * c + 128])
                moms.append(m[8 * s : 8 * s + 8, 128 * c : 128 * c + 128])
        done = len(tiles) // 3 if r < 7 else -(-len(tiles) // 3)
        for j in range((len(tiles) - 8) // 3, done):
            group = tiles[3 * j : 3 * j + 3] + [None] * (3 - len(tiles[3 * j : 3 * j + 3]))
            group += moms[3 * j : 3 * j + 3] + [None] * (3 - len(moms[3 * j : 3 * j + 3]))
            group = [jnp.zeros((8, 128), F32) if t is None else t for t in group]
            for q in range(3):
                pair = jnp.concatenate([group[2 * q], group[2 * q + 1]], axis=0)
                blocks[j, 16 * q : 16 * q + 16, :] = pair.astype(BF16)


def mean_kernel(matching, got, mean):
    for r in range(got.shape[0]):
        mine = got[r].astype(F32)
        theirs = got[matching[0, r]].astype(F32)
        mean[r] = (0.5 * (mine + theirs)).astype(BF16)


def outer_kernel(back, anchor, anchor_out, mom_out):
    for j in range(-(-64 // 3)):
        group = []
        for q in range(3):
            pair = back[j, 16 * q : 16 * q + 16, :].astype(F32)
            group += [pair[:8], pair[8:]]
        for t in range(3):
            tile = 3 * j + t
            if tile < 64:
                rows = slice(tile // 4 * 8, tile // 4 * 8 + 8)
                cols = slice(tile % 4 * 128, tile % 4 * 128 + 128)
                delta_avg, mom_avg = group[t], group[3 + t]
                mom_new = 0.5 * mom_avg + delta_avg
                mom_out[0, rows, cols] = mom_new
                anchor_out[0, rows, cols] = anchor[0, rows, cols] - 0.7 * (
                    0.5 * mom_new + delta_avg
                )


def join_kernel(w0, w2, w6, left, right):
    left[:256, :] = w0[...]
    left[256:, :] = w6[...]
    right[:256, :] = w0[...]
    right[256:, :] = w2[...]


def key_kernel(scale, own, other, w0, w2, w6, from_left, from_right, w4, mine, theirs):
    near, far = slice(0, 256), slice(256, 512)
    blocks = (
        (from_right, near), (from_right, far), (from_left, near), (from_left, far),
        (w4, near), (w2, near), (w6, near), (w0, near),
    )
    total_mine = jnp.zeros(mine.shape, F32)
    total_theirs = jnp.zeros(theirs.shape, F32)
    for p, (ref, rows) in enumerate(blocks):
        cols = slice(p * 256, p * 256 + 256)
        block = ref[rows, :]
        total_theirs += jnp.dot(other[:, cols], block, preferred_element_type=F32)
        total_mine += jnp.dot(own[:, cols], block, preferred_element_type=F32)
    mine[...] = scale * total_mine
    theirs[...] = (scale * total_theirs).astype(theirs.dtype)


def on_device(inputs, key_grad, weights, anchor, adam_first, adam_second, outer_mom, partner):
    scale = inputs.shape[1] ** (-0.5)
    replicas = lax.axis_size("rep")
    tokens = inputs.shape[0]
    work = 4 * tokens * inputs.shape[1] * key_grad.shape[1] // 2

    in_place = pltpu.with_memory_space_constraint(inputs, pltpu.HBM)
    away = pick(True, in_place, pltpu.with_memory_space_constraint(key_grad, pltpu.HBM))
    other = send(away, CORE)
    own = pick(False, in_place)
    packed, own = lax.optimization_barrier((weights[0].astype(BF16), own))
    w0 = jnp.concatenate([packed, send(packed, ZSWAP)], axis=0)

    def piece(rows, kind=BF16):
        return ((rows, 512), kind)

    a, b, c4, d2, d6, d0 = call(
        lambda *refs: grad_kernel(scale, *refs),
        (piece(512), piece(512), piece(256), piece(256, F32), piece(256, F32), piece(256, F32)),
        [VMEM] * 3, own, other, key_grad, flops=work,
    )
    a, b, c4 = send(a, ring(1)), send(b, ring(-1)), send(c4, ring(2))
    m2, m6 = call(relay_kernel, (piece(256), piece(256)), [VMEM] * 5, d2, d6, a, b, c4)
    w0, m2, m6 = lax.optimization_barrier((w0, m2, m6))
    e2, e6 = send(m2, ring(2)), send(m6, ring(-2))
    (far,) = call(far_kernel, (piece(128),), [VMEM] * 5, d0, a, b, e2, e6)
    far = send(far, ZSWAP)
    w6, w2 = send(w0, ring(2)), send(w0, ring(-2))
    w2, far, w6 = lax.optimization_barrier((w2, far, w6))
    shard = (weights.shape, F32)
    block = -(-64 // replicas) * 16
    first_new, second_new, blocks = call(
        adam_kernel, (shard, shard, ((replicas, block, 128), BF16)), [VMEM] * 11,
        d0, a, b, e2, e6, far, weights, anchor, adam_first, adam_second, outer_mom,
    )
    blocks, w0 = lax.optimization_barrier((blocks, w0))
    got = lax.all_to_all(blocks, "rep", split_axis=0, concat_axis=0, tiled=True)
    left, right = call(join_kernel, (piece(512), piece(512)), [VMEM] * 3, w0, w2, w6)
    from_left, from_right, w4 = send(left, ring(1)), send(right, ring(-1)), send(w6, ring(2))
    (mean,) = call(mean_kernel, ((got.shape, BF16),), [SMEM, VMEM], partner, got)
    back = lax.all_to_all(mean, "rep", split_axis=0, concat_axis=0, tiled=True)
    mine, theirs = call(
        lambda *refs: key_kernel(scale, *refs),
        (((tokens, 512), F32), ((tokens, 512), BF16)),
        [VMEM] * 8, own, other, w0, w2, w6, from_left, from_right, w4, flops=work,
    )
    keys = (mine + send(theirs, CORE).astype(F32)).astype(BF16)
    anchor_new, mom_new = call(outer_kernel, (shard, shard), [VMEM] * 2, back, anchor)
    return (keys, anchor_new, mom_new, first_new, second_new)


def solution(mesh):
    shard = P("rep", "fsdp", None)
    flat = P(("rep", "fsdp"), None)
    return jax.shard_map(
        on_device,
        mesh=mesh,
        in_specs=(flat, flat, shard, shard, shard, shard, shard, P("fsdp", None)),
        out_specs=(flat, shard, shard, shard, shard),
        check_vma=False,
    )
```

time: 333 us -> 135 us (0.41)
  the two profiles are of different devices: /device:TPU:1 before, /device:TPU:11 now
where the time goes in v2:
time: 135 us; the launch traced here: 134 us
  starting transfers between devices  83.9 us (62%)
  waiting for transfers between devices  37.4 us (28%)
  Pallas kernels  10.8 us (8%)
    ppermute x14, starting transfers between devices, send(): return lax.ppermute(value, 'fsdp', pairs)  61.6 us
    ppermute x14, waiting for transfers between devices, send(): return lax.ppermute(value, 'fsdp', pairs)  30 us
    all_to_all x1, starting transfers between devices, on_device(): got = lax.all_to_all(blocks, 'rep', split_axis=0, concat_axis=0, tiled=True)  14.9 us
    pallas_call x8, Pallas kernels, call(): pl.pallas_call(kernel, out_shape=tuple((jax.ShapeDtypeStruct(shape, kind)...  8.09 us
    all_to_all x1, starting transfers between devices, on_device(): back = lax.all_to_all(mean, 'rep', split_axis=0, concat_axis=0, tiled=True)  7.4 us
    all_to_all x1, waiting for transfers between devices, on_device(): got = lax.all_to_all(blocks, 'rep', split_axis=0, concat_axis=0, tiled=True)  7.36 us
  transfers between devices with their start and end apart: 16, of which 7 were waited for; matrix products, arithmetic and copies ran while one was open for 1% of the time, Pallas kernels for 4%

profile of v2, /device:TPU:11, one launch (start us, length us, event | category | flops | bytes accessed | tf_op | source)
XLA Modules:
  0.0 133.8 jit_solution(4881272002264125111)
XLA Ops:
  0.6 1.4 %shard_map.120 = bf16[192,2560]{1,0:T(8,128)(2,1)S(1)} custom-call(bf16[192,4096]{1,0:T(8,128)(2,1)} %refs_0_.3, bf16[192,512]{1,0:T(8,128)(2,1)} %refs_2_.1), custom_call_target="tpu_custom_call" | custom-call | tf_op jit(solution)/shard_map/pallas_call | solution.py:74
  2.0 2.7 %collective-permute-start = (bf16[192,2560]{1,0:T(8,128)(2,1)S(1)}, bf16[192,2560]{1,0:T(8,128)(2,1)S(1)}, u32[]{:S(2)}, u32[]{:S(2)}) collective-permute-start(bf16[192,2560]{1,0:T(8,128)(2,1)S(1)} %shard_map.120), channel_id=1, source_target_pairs={{0,1},{1,0},{2,3},{3,2},{4,5},{5,4},{6,7},{7,6},{8,9},{9,8},{10,11... | collective-permute-start | bytes 2949128 | tf_op jit(solution)/shard_map/ppermute | solution.py:38
  4.7 1.3 shard_map.119.refs_0_
  6.1 0.8 collective-permute-done.refs_1_
  6.9 1.3 shard_map.121
  8.2 2.1 %collective-permute-start.1 = (bf16[512,512]{1,0:T(8,128)(2,1)S(1)}, bf16[512,512]{1,0:T(8,128)(2,1)S(1)}, u32[]{:S(2)}, u32[]{:S(2)}) collective-permute-start(bf16[512,512]{1,0:T(8,128)(2,1)S(1)} %get-tuple-element.34), channel_id=1, source_target_pairs={{0,4},{1,29},{2,6},{3,31},{4,8},{5,1},{6,10},{7,3},{8,12},{9,5},{1... | collective-permute-start | bytes 1572872 | tf_op jit(solution)/shard_map/ppermute | solution.py:38
  10.3 3.2 %collective-permute-start.2 = (bf16[512,512]{1,0:T(8,128)(2,1)S(1)}, bf16[512,512]{1,0:T(8,128)(2,1)S(1)}, u32[]{:S(2)}, u32[]{:S(2)}) collective-permute-start(bf16[512,512]{1,0:T(8,128)(2,1)S(1)} %get-tuple-element.35), channel_id=1, source_target_pairs={{0,28},{1,5},{2,30},{3,7},{4,0},{5,9},{6,2},{7,11},{8,4},{9,13},{1... | collective-permute-start | bytes 1572872 | tf_op jit(solution)/shard_map/ppermute | solution.py:38
  13.5 6.2 %collective-permute-start.4 = (bf16[256,512]{1,0:T(8,128)(2,1)S(1)}, bf16[256,512]{1,0:T(8,128)(2,1)S(1)}, u32[]{:S(2)}, u32[]{:S(2)}) collective-permute-start(bf16[256,512]{1,0:T(8,128)(2,1)S(1)} %get-tuple-element.39), channel_id=1, source_target_pairs={{0,8},{1,25},{2,10},{3,27},{4,12},{5,29},{6,14},{7,31},{8,16},{9,1... | collective-permute-start | bytes 786440 | tf_op jit(solution)/shard_map/ppermute | solution.py:38
  19.7 14.9 %collective-permute-start.3 = (bf16[128,512]{1,0:T(8,128)(2,1)S(1)}, bf16[128,512]{1,0:T(8,128)(2,1)S(1)}, u32[]{:S(2)}, u32[]{:S(2)}) collective-permute-start(bf16[128,512]{1,0:T(8,128)(2,1)S(1)} %convert_bitcast_fusion), channel_id=1, source_target_pairs={{0,2},{1,3},{2,0},{3,1},{4,6},{5,7},{6,4},{7,5},{8,10},{9,11},{10,... | collective-permute-start | bytes 393224 | tf_op jit(solution)/shard_map/ppermute | solution.py:38
  34.6 3.8 %collective-permute-done.3 = bf16[128,512]{1,0:T(8,128)(2,1)S(1)} collective-permute-done((bf16[128,512]{1,0:T(8,128)(2,1)S(1)}, bf16[128,512]{1,0:T(8,128)(2,1)S(1)}, u32[]{:S(2)}, u32[]{:S(2)}) %collective-permute-start.3) | collective-permute-done | bytes 131104 | tf_op jit(solution)/shard_map/ppermute | solution.py:38
  38.6 2.8 %collective-permute-start.5 = (bf16[256,512]{1,0:T(8,128)(2,1)S(1)}, bf16[256,512]{1,0:T(8,128)(2,1)S(1)}, u32[]{:S(2)}, u32[]{:S(2)}) collective-permute-start(bf16[256,512]{1,0:T(8,128)(2,1)S(1)} %get-tuple-element.42), channel_id=1, source_target_pairs={{0,8},{1,25},{2,10},{3,27},{4,12},{5,29},{6,14},{7,31},{8,16},{9,1... | collective-permute-start | bytes 786440 | tf_op jit(solution)/shard_map/ppermute | solution.py:38
  41.5 3.5 %collective-permute-start.6 = (bf16[256,512]{1,0:T(8,128)(2,1)S(1)}, bf16[256,512]{1,0:T(8,128)(2,1)S(1)}, u32[]{:S(2)}, u32[]{:S(2)}) collective-permute-start(bf16[256,512]{1,0:T(8,128)(2,1)S(1)} %get-tuple-element.43), channel_id=1, source_target_pairs={{0,24},{1,9},{2,26},{3,11},{4,28},{5,13},{6,30},{7,15},{8,0},{9,17... | collective-permute-start | bytes 786440 | tf_op jit(solution)/shard_map/ppermute | solution.py:38
  45.0 3.9 %collective-permute-start.9 = (bf16[256,512]{1,0:T(8,128)(2,1)S(1)}, bf16[256,512]{1,0:T(8,128)(2,1)S(1)}, u32[]{:S(2)}, u32[]{:S(2)}) collective-permute-start(bf16[256,512]{1,0:T(8,128)(2,1)S(1)} %pad_maximum_fusion.w0.refs_2_), channel_id=1, source_target_pairs={{0,8},{1,25},{2,10},{3,27},{4,12},{5,29},{6,14},{7,31},{8,16},{9,1... | collective-permute-start | bytes 786440 | tf_op jit(solution)/shard_map/ppermute | solution.py:38
  48.9 2.3 %collective-permute-start.7 = (bf16[256,512]{1,0:T(8,128)(2,1)S(1)}, bf16[256,512]{1,0:T(8,128)(2,1)S(1)}, u32[]{:S(2)}, u32[]{:S(2)}) collective-permute-start(bf16[256,512]{1,0:T(8,128)(2,1)S(1)} %pad_maximum_fusion.w0.refs_2_), channel_id=1, source_target_pairs={{0,24},{1,9},{2,26},{3,11},{4,28},{5,13},{6,30},{7,15},{8,0},{9,17... | collective-permute-start | bytes 786440 | tf_op jit(solution)/shard_map/ppermute | solution.py:38
  51.2 12.1 %collective-permute-done.6.e6 = bf16[256,512]{1,0:T(8,128)(2,1)S(1)} collective-permute-done((bf16[256,512]{1,0:T(8,128)(2,1)S(1)}, bf16[256,512]{1,0:T(8,128)(2,1)S(1)}, u32[]{:S(2)}, u32[]{:S(2)}) %collective-permute-start.6) | collective-permute-done | bytes 262176 | tf_op jit(solution)/shard_map/ppermute | solution.py:38
  63.4 6.7 %collective-permute-start.8 = (bf16[128,512]{1,0:T(8,128)(2,1)S(1)}, bf16[128,512]{1,0:T(8,128)(2,1)S(1)}, u32[]{:S(2)}, u32[]{:S(2)}) collective-permute-start(bf16[128,512]{1,0:T(8,128)(2,1)S(1)} %shard_map.123), channel_id=1, source_target_pairs={{0,2},{1,3},{2,0},{3,1},{4,6},{5,7},{6,4},{7,5},{8,10},{9,11},{10,... | collective-permute-start | bytes 393224 | tf_op jit(solution)/shard_map/ppermute | solution.py:38
  70.1 6.3 %collective-permute-done.8.far = bf16[128,512]{1,0:T(8,128)(2,1)S(1)} collective-permute-done((bf16[128,512]{1,0:T(8,128)(2,1)S(1)}, bf16[128,512]{1,0:T(8,128)(2,1)S(1)}, u32[]{:S(2)}, u32[]{:S(2)}) %collective-permute-start.8) | collective-permute-done | bytes 131104 | tf_op jit(solution)/shard_map/ppermute | solution.py:38
  76.4 1.2 shard_map.124
  77.6 14.9 %all-to-all-start = ((bf16[24,48,128]{2,1,0:T(8,128)(2,1)}), bf16[24,48,128]{2,1,0:T(8,128)(2,1)S(1)}, u32[]{:S(2)}, u32[]{:S(2)}) async-start(bf16[24,48,128]{2,1,0:T(8,128)(2,1)} %get-tuple-element.54), calls=%async_computation | async-start | bytes 589824 | tf_op jit(solution)/shard_map/all_to_all | solution.py:235
  92.6 1.0 shard_map.125
  93.6 1.9 %collective-permute-start.10 = (bf16[512,512]{1,0:T(8,128)(2,1)}, bf16[512,512]{1,0:T(8,128)(2,1)}, u32[]{:S(2)}, u32[]{:S(2)}) collective-permute-start(bf16[512,512]{1,0:T(8,128)(2,1)} %get-tuple-element.50), channel_id=1, source_target_pairs={{0,4},{1,29},{2,6},{3,31},{4,8},{5,1},{6,10},{7,3},{8,12},{9,5},{1... | collective-permute-start | bytes 1572872 | tf_op jit(solution)/shard_map/ppermute | solution.py:38
  95.5 3.4 %collective-permute-start.11 = (bf16[512,512]{1,0:T(8,128)(2,1)}, bf16[512,512]{1,0:T(8,128)(2,1)}, u32[]{:S(2)}, u32[]{:S(2)}) collective-permute-start(bf16[512,512]{1,0:T(8,128)(2,1)} %get-tuple-element.51), channel_id=1, source_target_pairs={{0,28},{1,5},{2,30},{3,7},{4,0},{5,9},{6,2},{7,11},{8,4},{9,13},{1... | collective-permute-start | bytes 1572872 | tf_op jit(solution)/shard_map/ppermute | solution.py:38
  98.9 7.4 %all-to-all-done.got = bf16[24,48,128]{2,1,0:T(8,128)(2,1)S(1)} async-done(((bf16[24,48,128]{2,1,0:T(8,128)(2,1)}), bf16[24,48,128]{2,1,0:T(8,128)(2,1)S(1)}, u32[]{:S(2)}, u32[]{:S(2)}) %all-to-all-start) | async-done | bytes 294944 | tf_op jit(solution)/shard_map/all_to_all | solution.py:235
  106.2 1.4 %shard_map.127 = bf16[24,48,128]{2,1,0:T(8,128)(2,1)} custom-call(s32[1,24]{1,0:T(1,128)S(1)} %copy-done.6, bf16[24,48,128]{2,1,0:T(8,128)(2,1)S(1)} %all-to-all-done.got), custom_call_target="tpu_custom_call" | custom-call | bytes 1048576 | tf_op jit(solution)/shard_map/pallas_call | solution.py:85
  107.6 7.4 %all-to-all-start.1 = ((bf16[24,48,128]{2,1,0:T(8,128)(2,1)}), bf16[24,48,128]{2,1,0:T(8,128)(2,1)S(1)}, u32[]{:S(2)}, u32[]{:S(2)}) async-start(bf16[24,48,128]{2,1,0:T(8,128)(2,1)} %shard_map.127), calls=%async_computation.1 | async-start | bytes 589824 | tf_op jit(solution)/shard_map/all_to_all | solution.py:239
  115.0 2.4 %collective-permute-start.12 = (bf16[256,512]{1,0:T(8,128)(2,1)S(1)}, bf16[256,512]{1,0:T(8,128)(2,1)S(1)}, u32[]{:S(2)}, u32[]{:S(2)}) collective-permute-start(bf16[256,512]{1,0:T(8,128)(2,1)S(1)} %collective-permute-done.9.w6.refs_4_), channel_id=1, source_target_pairs={{0,8},{1,25},{2,10},{3,27},{4,12},{5,29},{6,14},{7,31},{8,16},{9,1... | collective-permute-start | bytes 786440 | tf_op jit(solution)/shard_map/ppermute | solution.py:38
  117.4 5.9 %collective-permute-done.12.refs_7_ = bf16[256,512]{1,0:T(8,128)(2,1)S(1)} collective-permute-done((bf16[256,512]{1,0:T(8,128)(2,1)S(1)}, bf16[256,512]{1,0:T(8,128)(2,1)S(1)}, u32[]{:S(2)}, u32[]{:S(2)}) %collective-permute-start.12) | collective-permute-done | bytes 262176 | tf_op jit(solution)/shard_map/ppermute | solution.py:38
  123.3 2.2 %shard_map.126 = (f32[192,512]{1,0:T(8,128)S(1)}, bf16[192,512]{1,0:T(8,128)(2,1)S(1)}) custom-call(bf16[192,2048]{1,0:T(8,128)(2,1)S(1)} %shard_map.119.refs_0_, bf16[192,2560]{1,0:T(8,128)(2,1)S(1)} %collective-permute-done.refs_1_, bf16[256,512]{1,0:T(8,128)(2,1)S(1)} %pad_maximum_fusion.w0.refs_2_, ...), custom_call_target="tpu_custom_call" | custom-call | flops 805306368 | bytes 1048576 | tf_op jit(solution)/shard_map/pallas_call | solution.py:85
  125.5 5.6 %collective-permute-start.13 = (bf16[192,512]{1,0:T(8,128)(2,1)S(1)}, bf16[192,512]{1,0:T(8,128)(2,1)S(1)}, u32[]{:S(2)}, u32[]{:S(2)}) collective-permute-start(bf16[192,512]{1,0:T(8,128)(2,1)S(1)} %get-tuple-element.53), channel_id=1, source_target_pairs={{0,1},{1,0},{2,3},{3,2},{4,5},{5,4},{6,7},{7,6},{8,9},{9,8},{10,11... | collective-permute-start | bytes 589832 | tf_op jit(solution)/shard_map/ppermute | solution.py:38
  131.2 1.0 collective-permute-done.13
  132.2 0.7 add_convert_fusion
  132.9 0.9 shard_map.128
  (27 shorter events, 0.3 us)
Async XLA Ops:
  2.0 4.1 %copy-start = (f32[1,128,512]{2,1,0:T(8,128)S(1)}, f32[1,128,512]{2,1,0:T(8,128)}, u32[]{:S(2)}) copy-start(f32[1,128,512]{2,1,0:T(8,128)} %weight.1) | copy-start | bytes 786436
  2.0 4.9 %copy-start.5 = (bf16[192,512]{1,0:T(8,128)(2,1)S(1)}, bf16[192,512]{1,0:T(8,128)(2,1)}, u32[]{:S(2)}) copy-start(bf16[192,512]{1,0:T(8,128)(2,1)} %refs_2_.1) | copy-start | bytes 589828
  2.0 4.9 %collective-permute-start = (bf16[192,2560]{1,0:T(8,128)(2,1)S(1)}, bf16[192,2560]{1,0:T(8,128)(2,1)S(1)}, u32[]{:S(2)}, u32[]{:S(2)}) collective-permute-start(bf16[192,2560]{1,0:T(8,128)(2,1)S(1)} %shard_map.120), channel_id=1, source_target_pairs={{0,1},{1,0},{2,3},{3,2},{4,5},{5,4},{6,7},{7,6},{8,9},{9,8},{10,11... | collective-permute-start | bytes 2949128 | tf_op jit(solution)/shard_map/ppermute | solution.py:38
  8.2 30.3 %collective-permute-start.1 = (bf16[512,512]{1,0:T(8,128)(2,1)S(1)}, bf16[512,512]{1,0:T(8,128)(2,1)S(1)}, u32[]{:S(2)}, u32[]{:S(2)}) collective-permute-start(bf16[512,512]{1,0:T(8,128)(2,1)S(1)} %get-tuple-element.34), channel_id=1, source_target_pairs={{0,4},{1,29},{2,6},{3,31},{4,8},{5,1},{6,10},{7,3},{8,12},{9,5},{1... | collective-permute-start | bytes 1572872 | tf_op jit(solution)/shard_map/ppermute | solution.py:38
  10.3 28.2 %collective-permute-start.2 = (bf16[512,512]{1,0:T(8,128)(2,1)S(1)}, bf16[512,512]{1,0:T(8,128)(2,1)S(1)}, u32[]{:S(2)}, u32[]{:S(2)}) collective-permute-start(bf16[512,512]{1,0:T(8,128)(2,1)S(1)} %get-tuple-element.35), channel_id=1, source_target_pairs={{0,28},{1,5},{2,30},{3,7},{4,0},{5,9},{6,2},{7,11},{8,4},{9,13},{1... | collective-permute-start | bytes 1572872 | tf_op jit(solution)/shard_map/ppermute | solution.py:38
  13.5 24.9 %collective-permute-start.4 = (bf16[256,512]{1,0:T(8,128)(2,1)S(1)}, bf16[256,512]{1,0:T(8,128)(2,1)S(1)}, u32[]{:S(2)}, u32[]{:S(2)}) collective-permute-start(bf16[256,512]{1,0:T(8,128)(2,1)S(1)} %get-tuple-element.39), channel_id=1, source_target_pairs={{0,8},{1,25},{2,10},{3,27},{4,12},{5,29},{6,14},{7,31},{8,16},{9,1... | collective-permute-start | bytes 786440 | tf_op jit(solution)/shard_map/ppermute | solution.py:38
  19.7 18.7 %collective-permute-start.3 = (bf16[128,512]{1,0:T(8,128)(2,1)S(1)}, bf16[128,512]{1,0:T(8,128)(2,1)S(1)}, u32[]{:S(2)}, u32[]{:S(2)}) collective-permute-start(bf16[128,512]{1,0:T(8,128)(2,1)S(1)} %convert_bitcast_fusion), channel_id=1, source_target_pairs={{0,2},{1,3},{2,0},{3,1},{4,6},{5,7},{6,4},{7,5},{8,10},{9,11},{10,... | collective-permute-start | bytes 393224 | tf_op jit(solution)/shard_map/ppermute | solution.py:38
  38.6 37.8 %copy-start.1 = (f32[1,128,512]{2,1,0:T(8,128)S(1)}, f32[1,128,512]{2,1,0:T(8,128)}, u32[]{:S(2)}) copy-start(f32[1,128,512]{2,1,0:T(8,128)} %anchor.3) | copy-start | bytes 786436
  38.6 37.8 %copy-start.2 = (f32[1,128,512]{2,1,0:T(8,128)S(1)}, f32[1,128,512]{2,1,0:T(8,128)}, u32[]{:S(2)}) copy-start(f32[1,128,512]{2,1,0:T(8,128)} %first.1) | copy-start | bytes 786436
  38.6 37.8 %copy-start.3 = (f32[1,128,512]{2,1,0:T(8,128)S(1)}, f32[1,128,512]{2,1,0:T(8,128)}, u32[]{:S(2)}) copy-start(f32[1,128,512]{2,1,0:T(8,128)} %second.1) | copy-start | bytes 786436
  38.6 37.8 %copy-start.4 = (f32[1,128,512]{2,1,0:T(8,128)S(1)}, f32[1,128,512]{2,1,0:T(8,128)}, u32[]{:S(2)}) copy-start(f32[1,128,512]{2,1,0:T(8,128)} %mom.1) | copy-start | bytes 786436
  38.6 12.5 %collective-permute-start.5 = (bf16[256,512]{1,0:T(8,128)(2,1)S(1)}, bf16[256,512]{1,0:T(8,128)(2,1)S(1)}, u32[]{:S(2)}, u32[]{:S(2)}) collective-permute-start(bf16[256,512]{1,0:T(8,128)(2,1)S(1)} %get-tuple-element.42), channel_id=1, source_target_pairs={{0,8},{1,25},{2,10},{3,27},{4,12},{5,29},{6,14},{7,31},{8,16},{9,1... | collective-permute-start | bytes 786440 | tf_op jit(solution)/shard_map/ppermute | solution.py:38
  41.5 21.8 %collective-permute-start.6 = (bf16[256,512]{1,0:T(8,128)(2,1)S(1)}, bf16[256,512]{1,0:T(8,128)(2,1)S(1)}, u32[]{:S(2)}, u32[]{:S(2)}) collective-permute-start(bf16[256,512]{1,0:T(8,128)(2,1)S(1)} %get-tuple-element.43), channel_id=1, source_target_pairs={{0,24},{1,9},{2,26},{3,11},{4,28},{5,13},{6,30},{7,15},{8,0},{9,17... | collective-permute-start | bytes 786440 | tf_op jit(solution)/shard_map/ppermute | solution.py:38
  45.0 25.1 %collective-permute-start.9 = (bf16[256,512]{1,0:T(8,128)(2,1)S(1)}, bf16[256,512]{1,0:T(8,128)(2,1)S(1)}, u32[]{:S(2)}, u32[]{:S(2)}) collective-permute-start(bf16[256,512]{1,0:T(8,128)(2,1)S(1)} %pad_maximum_fusion.w0.refs_2_), channel_id=1, source_target_pairs={{0,8},{1,25},{2,10},{3,27},{4,12},{5,29},{6,14},{7,31},{8,16},{9,1... | collective-permute-start | bytes 786440 | tf_op jit(solution)/shard_map/ppermute | solution.py:38
  48.9 21.2 %collective-permute-start.7 = (bf16[256,512]{1,0:T(8,128)(2,1)S(1)}, bf16[256,512]{1,0:T(8,128)(2,1)S(1)}, u32[]{:S(2)}, u32[]{:S(2)}) collective-permute-start(bf16[256,512]{1,0:T(8,128)(2,1)S(1)} %pad_maximum_fusion.w0.refs_2_), channel_id=1, source_target_pairs={{0,24},{1,9},{2,26},{3,11},{4,28},{5,13},{6,30},{7,15},{8,0},{9,17... | collective-permute-start | bytes 786440 | tf_op jit(solution)/shard_map/ppermute | solution.py:38
  63.4 42.8 %copy-start.6 = (s32[1,24]{1,0:T(1,128)S(1)}, s32[1,24]{1,0:T(1,128)}, u32[]{:S(2)}) copy-start(s32[1,24]{1,0:T(1,128)} %matching.1) | copy-start | bytes 292
  63.4 13.0 %collective-permute-start.8 = (bf16[128,512]{1,0:T(8,128)(2,1)S(1)}, bf16[128,512]{1,0:T(8,128)(2,1)S(1)}, u32[]{:S(2)}, u32[]{:S(2)}) collective-permute-start(bf16[128,512]{1,0:T(8,128)(2,1)S(1)} %shard_map.123), channel_id=1, source_target_pairs={{0,2},{1,3},{2,0},{3,1},{4,6},{5,7},{6,4},{7,5},{8,10},{9,11},{10,... | collective-permute-start | bytes 393224 | tf_op jit(solution)/shard_map/ppermute | solution.py:38
  77.6 28.6 %all-to-all-start = ((bf16[24,48,128]{2,1,0:T(8,128)(2,1)}), bf16[24,48,128]{2,1,0:T(8,128)(2,1)S(1)}, u32[]{:S(2)}, u32[]{:S(2)}) async-start(bf16[24,48,128]{2,1,0:T(8,128)(2,1)} %get-tuple-element.54), calls=%async_computation | async-start | bytes 589824 | tf_op jit(solution)/shard_map/all_to_all | solution.py:235
  93.6 29.7 %collective-permute-start.10 = (bf16[512,512]{1,0:T(8,128)(2,1)}, bf16[512,512]{1,0:T(8,128)(2,1)}, u32[]{:S(2)}, u32[]{:S(2)}) collective-permute-start(bf16[512,512]{1,0:T(8,128)(2,1)} %get-tuple-element.50), channel_id=1, source_target_pairs={{0,4},{1,29},{2,6},{3,31},{4,8},{5,1},{6,10},{7,3},{8,12},{9,5},{1... | collective-permute-start | bytes 1572872 | tf_op jit(solution)/shard_map/ppermute | solution.py:38
  95.5 27.8 %collective-permute-start.11 = (bf16[512,512]{1,0:T(8,128)(2,1)}, bf16[512,512]{1,0:T(8,128)(2,1)}, u32[]{:S(2)}, u32[]{:S(2)}) collective-permute-start(bf16[512,512]{1,0:T(8,128)(2,1)} %get-tuple-element.51), channel_id=1, source_target_pairs={{0,28},{1,5},{2,30},{3,7},{4,0},{5,9},{6,2},{7,11},{8,4},{9,13},{1... | collective-permute-start | bytes 1572872 | tf_op jit(solution)/shard_map/ppermute | solution.py:38
  107.6 25.3 %all-to-all-start.1 = ((bf16[24,48,128]{2,1,0:T(8,128)(2,1)}), bf16[24,48,128]{2,1,0:T(8,128)(2,1)S(1)}, u32[]{:S(2)}, u32[]{:S(2)}) async-start(bf16[24,48,128]{2,1,0:T(8,128)(2,1)} %shard_map.127), calls=%async_computation.1 | async-start | bytes 589824 | tf_op jit(solution)/shard_map/all_to_all | solution.py:239
  115.0 8.3 %collective-permute-start.12 = (bf16[256,512]{1,0:T(8,128)(2,1)S(1)}, bf16[256,512]{1,0:T(8,128)(2,1)S(1)}, u32[]{:S(2)}, u32[]{:S(2)}) collective-permute-start(bf16[256,512]{1,0:T(8,128)(2,1)S(1)} %collective-permute-done.9.w6.refs_4_), channel_id=1, source_target_pairs={{0,8},{1,25},{2,10},{3,27},{4,12},{5,29},{6,14},{7,31},{8,16},{9,1... | collective-permute-start | bytes 786440 | tf_op jit(solution)/shard_map/ppermute | solution.py:38
  125.5 6.7 %collective-permute-start.13 = (bf16[192,512]{1,0:T(8,128)(2,1)S(1)}, bf16[192,512]{1,0:T(8,128)(2,1)S(1)}, u32[]{:S(2)}, u32[]{:S(2)}) collective-permute-start(bf16[192,512]{1,0:T(8,128)(2,1)S(1)} %get-tuple-element.53), channel_id=1, source_target_pairs={{0,1},{1,0},{2,3},{3,2},{4,5},{5,4},{6,7},{7,6},{8,9},{9,8},{10,11... | collective-permute-start | bytes 589832 | tf_op jit(solution)/shard_map/ppermute | solution.py:38

commit v3 on v2

--- a/solution.py
+++ b/solution.py
@@ -179,21 +179,31 @@
     right[256:, :] = w2[...]
 
 
-def key_kernel(scale, own, other, w0, w2, w6, from_left, from_right, w4, mine, theirs):
+def key_kernel(own, other, w0, w2, w6, from_left, from_right, mine, theirs):
     near, far = slice(0, 256), slice(256, 512)
     blocks = (
         (from_right, near), (from_right, far), (from_left, near), (from_left, far),
-        (w4, near), (w2, near), (w6, near), (w0, near),
+        None, (w2, near), (w6, near), (w0, near),
     )
     total_mine = jnp.zeros(mine.shape, F32)
     total_theirs = jnp.zeros(theirs.shape, F32)
-    for p, (ref, rows) in enumerate(blocks):
-        cols = slice(p * 256, p * 256 + 256)
-        block = ref[rows, :]
-        total_theirs += jnp.dot(other[:, cols], block, preferred_element_type=F32)
-        total_mine += jnp.dot(own[:, cols], block, preferred_element_type=F32)
-    mine[...] = scale * total_mine
-    theirs[...] = (scale * total_theirs).astype(theirs.dtype)
+    for p, place in enumerate(blocks):
+        if place is not None:
+            cols = slice(p * 256, p * 256 + 256)
+            block = place[0][place[1], :]
+            total_theirs += jnp.dot(other[:, cols], block, preferred_element_type=F32)
+            total_mine += jnp.dot(own[:, cols], block, preferred_element_type=F32)
+    mine[...] = total_mine
+    theirs[...] = total_theirs
+
+
+def last_key_kernel(scale, own, other, w4, mine_in, theirs_in, mine, theirs):
+    cols = slice(1024, 1280)
+    block = w4[...]
+    part = theirs_in[...] + jnp.dot(other[:, cols], block, preferred_element_type=F32)
+    theirs[...] = (scale * part).astype(theirs.dtype)
+    part = mine_in[...] + jnp.dot(own[:, cols], block, preferred_element_type=F32)
+    mine[...] = scale * part
 
 
 def on_device(inputs, key_grad, weights, anchor, adam_first, adam_second, outer_mom, partner):
@@ -219,7 +229,6 @@
     )
     a, b, c4 = send(a, ring(1)), send(b, ring(-1)), send(c4, ring(2))
     m2, m6 = call(relay_kernel, (piece(256), piece(256)), [VMEM] * 5, d2, d6, a, b, c4)
-    w0, m2, m6 = lax.optimization_barrier((w0, m2, m6))
     e2, e6 = send(m2, ring(2)), send(m6, ring(-2))
     (far,) = call(far_kernel, (piece(128),), [VMEM] * 5, d0, a, b, e2, e6)
     far = send(far, ZSWAP)
@@ -237,10 +246,14 @@
     from_left, from_right, w4 = send(left, ring(1)), send(right, ring(-1)), send(w6, ring(2))
     (mean,) = call(mean_kernel, ((got.shape, BF16),), [SMEM, VMEM], partner, got)
     back = lax.all_to_all(mean, "rep", split_axis=0, concat_axis=0, tiled=True)
+    partial = ((tokens, 512), F32)
     mine, theirs = call(
-        lambda *refs: key_kernel(scale, *refs),
-        (((tokens, 512), F32), ((tokens, 512), BF16)),
-        [VMEM] * 8, own, other, w0, w2, w6, from_left, from_right, w4, flops=work,
+        key_kernel, (partial, partial),
+        [VMEM] * 7, own, other, w0, w2, w6, from_left, from_right, flops=work,
+    )
+    mine, theirs = call(
+        lambda *refs: last_key_kernel(scale, *refs), (partial, ((tokens, 512), BF16)),
+        [VMEM] * 5, own, other, w4, mine, theirs, flops=work // 8,
     )
     keys = (mine + send(theirs, CORE).astype(F32)).astype(BF16)
     anchor_new, mom_new = call(outer_kernel, (shard, shard), [VMEM] * 2, back, anchor)

time: 135 us -> 129 us (0.956)
  the two profiles are of different devices: /device:TPU:11 before, /device:TPU:43 now
where the time goes in v3:
time: 129 us; the launch traced here: 128 us
  starting transfers between devices  88.9 us (69%)
  waiting for transfers between devices  26.3 us (20%)
  Pallas kernels  10.9 us (8%)
    ppermute x14, starting transfers between devices, send(): return lax.ppermute(value, 'fsdp', pairs)  71.9 us
    ppermute x14, waiting for transfers between devices, send(): return lax.ppermute(value, 'fsdp', pairs)  19 us
    all_to_all x1, starting transfers between devices, on_device(): got = lax.all_to_all(blocks, 'rep', split_axis=0, concat_axis=0, tiled=True)  9.65 us
    pallas_call x9, Pallas kernels, call(): pl.pallas_call(kernel, out_shape=tuple((jax.ShapeDtypeStruct(shape, kind)...  8.26 us
    all_to_all x1, starting transfers between devices, on_device(): back = lax.all_to_all(mean, 'rep', split_axis=0, concat_axis=0, tiled=True)  7.4 us
    all_to_all x1, waiting for transfers between devices, on_device(): got = lax.all_to_all(blocks, 'rep', split_axis=0, concat_axis=0, tiled=True)  7.34 us
    pallas_call x2, Pallas kernels, pick(): pl.pallas_call(lambda *refs: pick_kernel(away, *refs), out_shape=jax.Shap...  2.68 us
  transfers between devices with their start and end apart: 16, of which 6 were waited for; matrix products, arithmetic and copies ran while one was open for 1% of the time, Pallas kernels for 5%

profile of v3, /device:TPU:43, one launch (start us, length us, event | category | flops | bytes accessed | tf_op | source)
XLA Modules:
  0.0 128.0 jit_solution(570446428256218386)
XLA Ops:
  0.6 1.4 %shard_map.120 = bf16[192,2560]{1,0:T(8,128)(2,1)S(1)} custom-call(bf16[192,4096]{1,0:T(8,128)(2,1)} %refs_0_.3, bf16[192,512]{1,0:T(8,128)(2,1)} %refs_2_.1), custom_call_target="tpu_custom_call" | custom-call | tf_op jit(solution)/shard_map/pallas_call | solution.py:74
  2.0 2.7 %collective-permute-start = (bf16[192,2560]{1,0:T(8,128)(2,1)S(1)}, bf16[192,2560]{1,0:T(8,128)(2,1)S(1)}, u32[]{:S(2)}, u32[]{:S(2)}) collective-permute-start(bf16[192,2560]{1,0:T(8,128)(2,1)S(1)} %shard_map.120), channel_id=1, source_target_pairs={{0,1},{1,0},{2,3},{3,2},{4,5},{5,4},{6,7},{7,6},{8,9},{9,8},{10,11... | collective-permute-start | bytes 2949128 | tf_op jit(solution)/shard_map/ppermute | solution.py:38
  4.7 1.3 %shard_map.119.refs_0_.own = bf16[192,2048]{1,0:T(8,128)(2,1)S(1)} custom-call(bf16[192,4096]{1,0:T(8,128)(2,1)} %refs_0_.3), custom_call_target="tpu_custom_call" | custom-call | tf_op jit(solution)/shard_map/pallas_call | solution.py:74
  6.1 0.8 collective-permute-done.refs_1_.other
  6.9 1.3 %shard_map.121 = (bf16[512,512]{1,0:T(8,128)(2,1)S(1)}, bf16[512,512]{1,0:T(8,128)(2,1)S(1)}, bf16[256,512]{1,0:T(8,128)(2,1)S(1)}, f32[256,512]{1,0:T(8,128)S(1...) custom-call(bf16[192,2048]{1,0:T(8,128)(2,1)S(1)} %shard_map.119.refs_0_.own, ...), custom_call_target="tpu_custom_call" | custom-call | flops 805306368 | bytes 1048576 | tf_op jit(solution)/shard_map/pallas_call | solution.py:85
  8.2 3.0 %collective-permute-start.3 = (bf16[512,512]{1,0:T(8,128)(2,1)S(1)}, bf16[512,512]{1,0:T(8,128)(2,1)S(1)}, u32[]{:S(2)}, u32[]{:S(2)}) collective-permute-start(bf16[512,512]{1,0:T(8,128)(2,1)S(1)} %get-tuple-element.34), channel_id=1, source_target_pairs={{0,4},{1,29},{2,6},{3,31},{4,8},{5,1},{6,10},{7,3},{8,12},{9,5},{1... | collective-permute-start | bytes 1572872 | tf_op jit(solution)/shard_map/ppermute | solution.py:38
  11.2 2.3 %collective-permute-start.4 = (bf16[512,512]{1,0:T(8,128)(2,1)S(1)}, bf16[512,512]{1,0:T(8,128)(2,1)S(1)}, u32[]{:S(2)}, u32[]{:S(2)}) collective-permute-start(bf16[512,512]{1,0:T(8,128)(2,1)S(1)} %get-tuple-element.35), channel_id=1, source_target_pairs={{0,28},{1,5},{2,30},{3,7},{4,0},{5,9},{6,2},{7,11},{8,4},{9,13},{1... | collective-permute-start | bytes 1572872 | tf_op jit(solution)/shard_map/ppermute | solution.py:38
  13.5 4.1 %collective-permute-start.5 = (bf16[256,512]{1,0:T(8,128)(2,1)S(1)}, bf16[256,512]{1,0:T(8,128)(2,1)S(1)}, u32[]{:S(2)}, u32[]{:S(2)}) collective-permute-start(bf16[256,512]{1,0:T(8,128)(2,1)S(1)} %get-tuple-element.38), channel_id=1, source_target_pairs={{0,8},{1,25},{2,10},{3,27},{4,12},{5,29},{6,14},{7,31},{8,16},{9,1... | collective-permute-start | bytes 786440 | tf_op jit(solution)/shard_map/ppermute | solution.py:38
  17.6 14.9 %collective-permute-start.1 = (bf16[128,512]{1,0:T(8,128)(2,1)S(1)}, bf16[128,512]{1,0:T(8,128)(2,1)S(1)}, u32[]{:S(2)}, u32[]{:S(2)}) collective-permute-start(bf16[128,512]{1,0:T(8,128)(2,1)S(1)} %convert_bitcast_fusion), channel_id=1, source_target_pairs={{0,2},{1,3},{2,0},{3,1},{4,6},{5,7},{6,4},{7,5},{8,10},{9,11},{10,... | collective-permute-start | bytes 393224 | tf_op jit(solution)/shard_map/ppermute | solution.py:38
  32.7 2.1 %collective-permute-start.6 = (bf16[256,512]{1,0:T(8,128)(2,1)S(1)}, bf16[256,512]{1,0:T(8,128)(2,1)S(1)}, u32[]{:S(2)}, u32[]{:S(2)}) collective-permute-start(bf16[256,512]{1,0:T(8,128)(2,1)S(1)} %get-tuple-element.39), channel_id=1, source_target_pairs={{0,8},{1,25},{2,10},{3,27},{4,12},{5,29},{6,14},{7,31},{8,16},{9,1... | collective-permute-start | bytes 786440 | tf_op jit(solution)/shard_map/ppermute | solution.py:38
  34.7 4.3 %collective-permute-start.7 = (bf16[256,512]{1,0:T(8,128)(2,1)S(1)}, bf16[256,512]{1,0:T(8,128)(2,1)S(1)}, u32[]{:S(2)}, u32[]{:S(2)}) collective-permute-start(bf16[256,512]{1,0:T(8,128)(2,1)S(1)} %get-tuple-element.40), channel_id=1, source_target_pairs={{0,24},{1,9},{2,26},{3,11},{4,28},{5,13},{6,30},{7,15},{8,0},{9,17... | collective-permute-start | bytes 786440 | tf_op jit(solution)/shard_map/ppermute | solution.py:38
  39.0 3.3 %collective-permute-start.2 = (bf16[256,512]{1,0:T(8,128)(2,1)S(1)}, bf16[256,512]{1,0:T(8,128)(2,1)S(1)}, u32[]{:S(2)}, u32[]{:S(2)}) collective-permute-start(bf16[256,512]{1,0:T(8,128)(2,1)S(1)} %constant_dynamic-update-slice_fusion.w0), channel_id=1, source_target_pairs={{0,24},{1,9},{2,26},{3,11},{4,28},{5,13},{6,30},{7,15},{8,0},{9,17... | collective-permute-start | bytes 786440 | tf_op jit(solution)/shard_map/ppermute | solution.py:38
  42.4 4.1 %collective-permute-start.9 = (bf16[256,512]{1,0:T(8,128)(2,1)S(1)}, bf16[256,512]{1,0:T(8,128)(2,1)S(1)}, u32[]{:S(2)}, u32[]{:S(2)}) collective-permute-start(bf16[256,512]{1,0:T(8,128)(2,1)S(1)} %constant_dynamic-update-slice_fusion.w0), channel_id=1, source_target_pairs={{0,8},{1,25},{2,10},{3,27},{4,12},{5,29},{6,14},{7,31},{8,16},{9,1... | collective-permute-start | bytes 786440 | tf_op jit(solution)/shard_map/ppermute | solution.py:38
  46.5 4.4 %collective-permute-done.7.e6 = bf16[256,512]{1,0:T(8,128)(2,1)S(1)} collective-permute-done((bf16[256,512]{1,0:T(8,128)(2,1)S(1)}, bf16[256,512]{1,0:T(8,128)(2,1)S(1)}, u32[]{:S(2)}, u32[]{:S(2)}) %collective-permute-start.7) | collective-permute-done | bytes 262176 | tf_op jit(solution)/shard_map/ppermute | solution.py:38
  51.0 18.1 %collective-permute-start.8 = (bf16[128,512]{1,0:T(8,128)(2,1)S(1)}, bf16[128,512]{1,0:T(8,128)(2,1)S(1)}, u32[]{:S(2)}, u32[]{:S(2)}) collective-permute-start(bf16[128,512]{1,0:T(8,128)(2,1)S(1)} %shard_map.123), channel_id=1, source_target_pairs={{0,2},{1,3},{2,0},{3,1},{4,6},{5,7},{6,4},{7,5},{8,10},{9,11},{10,... | collective-permute-start | bytes 393224 | tf_op jit(solution)/shard_map/ppermute | solution.py:38
  69.1 8.4 %collective-permute-done.8.far = bf16[128,512]{1,0:T(8,128)(2,1)S(1)} collective-permute-done((bf16[128,512]{1,0:T(8,128)(2,1)S(1)}, bf16[128,512]{1,0:T(8,128)(2,1)S(1)}, u32[]{:S(2)}, u32[]{:S(2)}) %collective-permute-start.8) | collective-permute-done | bytes 131104 | tf_op jit(solution)/shard_map/ppermute | solution.py:38
  77.5 1.2 shard_map.124
  78.7 9.6 %all-to-all-start = ((bf16[24,48,128]{2,1,0:T(8,128)(2,1)}), bf16[24,48,128]{2,1,0:T(8,128)(2,1)S(1)}, u32[]{:S(2)}, u32[]{:S(2)}) async-start(bf16[24,48,128]{2,1,0:T(8,128)(2,1)} %get-tuple-element.52), calls=%async_computation | async-start | bytes 589824 | tf_op jit(solution)/shard_map/all_to_all | solution.py:244
  88.3 1.0 shard_map.125
  89.4 1.9 %collective-permute-start.11 = (bf16[512,512]{1,0:T(8,128)(2,1)}, bf16[512,512]{1,0:T(8,128)(2,1)}, u32[]{:S(2)}, u32[]{:S(2)}) collective-permute-start(bf16[512,512]{1,0:T(8,128)(2,1)} %get-tuple-element.46), channel_id=1, source_target_pairs={{0,4},{1,29},{2,6},{3,31},{4,8},{5,1},{6,10},{7,3},{8,12},{9,5},{1... | collective-permute-start | bytes 1572872 | tf_op jit(solution)/shard_map/ppermute | solution.py:38
  91.3 3.4 %collective-permute-start.12 = (bf16[512,512]{1,0:T(8,128)(2,1)}, bf16[512,512]{1,0:T(8,128)(2,1)}, u32[]{:S(2)}, u32[]{:S(2)}) collective-permute-start(bf16[512,512]{1,0:T(8,128)(2,1)} %get-tuple-element.47), channel_id=1, source_target_pairs={{0,28},{1,5},{2,30},{3,7},{4,0},{5,9},{6,2},{7,11},{8,4},{9,13},{1... | collective-permute-start | bytes 1572872 | tf_op jit(solution)/shard_map/ppermute | solution.py:38
  94.7 7.3 %all-to-all-done.got = bf16[24,48,128]{2,1,0:T(8,128)(2,1)S(1)} async-done(((bf16[24,48,128]{2,1,0:T(8,128)(2,1)}), bf16[24,48,128]{2,1,0:T(8,128)(2,1)S(1)}, u32[]{:S(2)}, u32[]{:S(2)}) %all-to-all-start) | async-done | bytes 294944 | tf_op jit(solution)/shard_map/all_to_all | solution.py:244
  102.0 1.4 %shard_map.128 = bf16[24,48,128]{2,1,0:T(8,128)(2,1)} custom-call(s32[1,24]{1,0:T(1,128)S(1)} %copy-done.6, bf16[24,48,128]{2,1,0:T(8,128)(2,1)S(1)} %all-to-all-done.got), custom_call_target="tpu_custom_call" | custom-call | bytes 1048576 | tf_op jit(solution)/shard_map/pallas_call | solution.py:85
  103.3 7.4 %all-to-all-start.1 = ((bf16[24,48,128]{2,1,0:T(8,128)(2,1)}), bf16[24,48,128]{2,1,0:T(8,128)(2,1)S(1)}, u32[]{:S(2)}, u32[]{:S(2)}) async-start(bf16[24,48,128]{2,1,0:T(8,128)(2,1)} %shard_map.128), calls=%async_computation.1 | async-start | bytes 589824 | tf_op jit(solution)/shard_map/all_to_all | solution.py:248
  110.8 1.9 %collective-permute-start.10 = (bf16[256,512]{1,0:T(8,128)(2,1)S(1)}, bf16[256,512]{1,0:T(8,128)(2,1)S(1)}, u32[]{:S(2)}, u32[]{:S(2)}) collective-permute-start(bf16[256,512]{1,0:T(8,128)(2,1)S(1)} %collective-permute-done.9.w6), channel_id=1, source_target_pairs={{0,8},{1,25},{2,10},{3,27},{4,12},{5,29},{6,14},{7,31},{8,16},{9,1... | collective-permute-start | bytes 786440 | tf_op jit(solution)/shard_map/ppermute | solution.py:38
  112.7 2.1 %shard_map.126 = (f32[192,512]{1,0:T(8,128)S(1)}, f32[192,512]{1,0:T(8,128)S(1)}) custom-call(bf16[192,2048]{1,0:T(8,128)(2,1)S(1)} %shard_map.119.refs_0_.own, bf16[192,2560]{1,0:T(8,128)(2,1)S(1)} %collective-permute-done.refs_1_.other, bf16[256,512]{1,0:T(8,128)(2,1)S(1)} %constant_dynamic-update-slice_fusion.w0, ...), custom_call_target="tpu_custom_call" | custom-call | flops 805306368 | bytes 1048576 | tf_op jit(solution)/shard_map/pallas_call | solution.py:85
  114.8 4.3 %collective-permute-done.10.refs_2_ = bf16[256,512]{1,0:T(8,128)(2,1)S(1)} collective-permute-done((bf16[256,512]{1,0:T(8,128)(2,1)S(1)}, bf16[256,512]{1,0:T(8,128)(2,1)S(1)}, u32[]{:S(2)}, u32[]{:S(2)}) %collective-permute-start.10) | collective-permute-done | bytes 262176 | tf_op jit(solution)/shard_map/ppermute | solution.py:38
  119.1 0.3 shard_map.127
  119.3 6.0 %collective-permute-start.13 = (bf16[192,512]{1,0:T(8,128)(2,1)S(1)}, bf16[192,512]{1,0:T(8,128)(2,1)S(1)}, u32[]{:S(2)}, u32[]{:S(2)}) collective-permute-start(bf16[192,512]{1,0:T(8,128)(2,1)S(1)} %get-tuple-element.51), channel_id=1, source_target_pairs={{0,1},{1,0},{2,3},{3,2},{4,5},{5,4},{6,7},{7,6},{8,9},{9,8},{10,11... | collective-permute-start | bytes 589832 | tf_op jit(solution)/shard_map/ppermute | solution.py:38
  125.3 1.0 collective-permute-done.13
  126.4 0.7 add_convert_fusion
  127.1 0.9 shard_map.129
  (29 shorter events, 0.3 us)
Async XLA Ops:
  2.0 4.1 %copy-start = (f32[1,128,512]{2,1,0:T(8,128)S(1)}, f32[1,128,512]{2,1,0:T(8,128)}, u32[]{:S(2)}) copy-start(f32[1,128,512]{2,1,0:T(8,128)} %weight.1) | copy-start | bytes 786436
  2.0 4.9 %copy-start.5 = (bf16[192,512]{1,0:T(8,128)(2,1)S(1)}, bf16[192,512]{1,0:T(8,128)(2,1)}, u32[]{:S(2)}) copy-start(bf16[192,512]{1,0:T(8,128)(2,1)} %refs_2_.1) | copy-start | bytes 589828
  2.0 4.9 %collective-permute-start = (bf16[192,2560]{1,0:T(8,128)(2,1)S(1)}, bf16[192,2560]{1,0:T(8,128)(2,1)S(1)}, u32[]{:S(2)}, u32[]{:S(2)}) collective-permute-start(bf16[192,2560]{1,0:T(8,128)(2,1)S(1)} %shard_map.120), channel_id=1, source_target_pairs={{0,1},{1,0},{2,3},{3,2},{4,5},{5,4},{6,7},{7,6},{8,9},{9,8},{10,11... | collective-permute-start | bytes 2949128 | tf_op jit(solution)/shard_map/ppermute | solution.py:38
  8.2 24.3 %collective-permute-start.3 = (bf16[512,512]{1,0:T(8,128)(2,1)S(1)}, bf16[512,512]{1,0:T(8,128)(2,1)S(1)}, u32[]{:S(2)}, u32[]{:S(2)}) collective-permute-start(bf16[512,512]{1,0:T(8,128)(2,1)S(1)} %get-tuple-element.34), channel_id=1, source_target_pairs={{0,4},{1,29},{2,6},{3,31},{4,8},{5,1},{6,10},{7,3},{8,12},{9,5},{1... | collective-permute-start | bytes 1572872 | tf_op jit(solution)/shard_map/ppermute | solution.py:38
  11.2 21.3 %collective-permute-start.4 = (bf16[512,512]{1,0:T(8,128)(2,1)S(1)}, bf16[512,512]{1,0:T(8,128)(2,1)S(1)}, u32[]{:S(2)}, u32[]{:S(2)}) collective-permute-start(bf16[512,512]{1,0:T(8,128)(2,1)S(1)} %get-tuple-element.35), channel_id=1, source_target_pairs={{0,28},{1,5},{2,30},{3,7},{4,0},{5,9},{6,2},{7,11},{8,4},{9,13},{1... | collective-permute-start | bytes 1572872 | tf_op jit(solution)/shard_map/ppermute | solution.py:38
  13.5 19.0 %collective-permute-start.5 = (bf16[256,512]{1,0:T(8,128)(2,1)S(1)}, bf16[256,512]{1,0:T(8,128)(2,1)S(1)}, u32[]{:S(2)}, u32[]{:S(2)}) collective-permute-start(bf16[256,512]{1,0:T(8,128)(2,1)S(1)} %get-tuple-element.38), channel_id=1, source_target_pairs={{0,8},{1,25},{2,10},{3,27},{4,12},{5,29},{6,14},{7,31},{8,16},{9,1... | collective-permute-start | bytes 786440 | tf_op jit(solution)/shard_map/ppermute | solution.py:38
  17.6 21.4 %collective-permute-start.1 = (bf16[128,512]{1,0:T(8,128)(2,1)S(1)}, bf16[128,512]{1,0:T(8,128)(2,1)S(1)}, u32[]{:S(2)}, u32[]{:S(2)}) collective-permute-start(bf16[128,512]{1,0:T(8,128)(2,1)S(1)} %convert_bitcast_fusion), channel_id=1, source_target_pairs={{0,2},{1,3},{2,0},{3,1},{4,6},{5,7},{6,4},{7,5},{8,10},{9,11},{10,... | collective-permute-start | bytes 393224 | tf_op jit(solution)/shard_map/ppermute | solution.py:38
  32.6 44.9 %copy-start.1 = (f32[1,128,512]{2,1,0:T(8,128)S(1)}, f32[1,128,512]{2,1,0:T(8,128)}, u32[]{:S(2)}) copy-start(f32[1,128,512]{2,1,0:T(8,128)} %anchor.3) | copy-start | bytes 786436
  32.6 44.8 %copy-start.2 = (f32[1,128,512]{2,1,0:T(8,128)S(1)}, f32[1,128,512]{2,1,0:T(8,128)}, u32[]{:S(2)}) copy-start(f32[1,128,512]{2,1,0:T(8,128)} %first.1) | copy-start | bytes 786436
  32.6 44.8 %copy-start.3 = (f32[1,128,512]{2,1,0:T(8,128)S(1)}, f32[1,128,512]{2,1,0:T(8,128)}, u32[]{:S(2)}) copy-start(f32[1,128,512]{2,1,0:T(8,128)} %second.1) | copy-start | bytes 786436
  32.7 44.8 %copy-start.4 = (f32[1,128,512]{2,1,0:T(8,128)S(1)}, f32[1,128,512]{2,1,0:T(8,128)}, u32[]{:S(2)}) copy-start(f32[1,128,512]{2,1,0:T(8,128)} %mom.1) | copy-start | bytes 786436
  32.7 13.8 %collective-permute-start.6 = (bf16[256,512]{1,0:T(8,128)(2,1)S(1)}, bf16[256,512]{1,0:T(8,128)(2,1)S(1)}, u32[]{:S(2)}, u32[]{:S(2)}) collective-permute-start(bf16[256,512]{1,0:T(8,128)(2,1)S(1)} %get-tuple-element.39), channel_id=1, source_target_pairs={{0,8},{1,25},{2,10},{3,27},{4,12},{5,29},{6,14},{7,31},{8,16},{9,1... | collective-permute-start | bytes 786440 | tf_op jit(solution)/shard_map/ppermute | solution.py:38
  34.7 16.1 %collective-permute-start.7 = (bf16[256,512]{1,0:T(8,128)(2,1)S(1)}, bf16[256,512]{1,0:T(8,128)(2,1)S(1)}, u32[]{:S(2)}, u32[]{:S(2)}) collective-permute-start(bf16[256,512]{1,0:T(8,128)(2,1)S(1)} %get-tuple-element.40), channel_id=1, source_target_pairs={{0,24},{1,9},{2,26},{3,11},{4,28},{5,13},{6,30},{7,15},{8,0},{9,17... | collective-permute-start | bytes 786440 | tf_op jit(solution)/shard_map/ppermute | solution.py:38
  39.0 30.0 %collective-permute-start.2 = (bf16[256,512]{1,0:T(8,128)(2,1)S(1)}, bf16[256,512]{1,0:T(8,128)(2,1)S(1)}, u32[]{:S(2)}, u32[]{:S(2)}) collective-permute-start(bf16[256,512]{1,0:T(8,128)(2,1)S(1)} %constant_dynamic-update-slice_fusion.w0), channel_id=1, source_target_pairs={{0,24},{1,9},{2,26},{3,11},{4,28},{5,13},{6,30},{7,15},{8,0},{9,17... | collective-permute-start | bytes 786440 | tf_op jit(solution)/shard_map/ppermute | solution.py:38
  42.4 26.7 %collective-permute-start.9 = (bf16[256,512]{1,0:T(8,128)(2,1)S(1)}, bf16[256,512]{1,0:T(8,128)(2,1)S(1)}, u32[]{:S(2)}, u32[]{:S(2)}) collective-permute-start(bf16[256,512]{1,0:T(8,128)(2,1)S(1)} %constant_dynamic-update-slice_fusion.w0), channel_id=1, source_target_pairs={{0,8},{1,25},{2,10},{3,27},{4,12},{5,29},{6,14},{7,31},{8,16},{9,1... | collective-permute-start | bytes 786440 | tf_op jit(solution)/shard_map/ppermute | solution.py:38
  51.0 51.0 %copy-start.6 = (s32[1,24]{1,0:T(1,128)S(1)}, s32[1,24]{1,0:T(1,128)}, u32[]{:S(2)}) copy-start(s32[1,24]{1,0:T(1,128)} %matching.1) | copy-start | bytes 292
  51.0 26.5 %collective-permute-start.8 = (bf16[128,512]{1,0:T(8,128)(2,1)S(1)}, bf16[128,512]{1,0:T(8,128)(2,1)S(1)}, u32[]{:S(2)}, u32[]{:S(2)}) collective-permute-start(bf16[128,512]{1,0:T(8,128)(2,1)S(1)} %shard_map.123), channel_id=1, source_target_pairs={{0,2},{1,3},{2,0},{3,1},{4,6},{5,7},{6,4},{7,5},{8,10},{9,11},{10,... | collective-permute-start | bytes 393224 | tf_op jit(solution)/shard_map/ppermute | solution.py:38
  78.7 23.3 %all-to-all-start = ((bf16[24,48,128]{2,1,0:T(8,128)(2,1)}), bf16[24,48,128]{2,1,0:T(8,128)(2,1)S(1)}, u32[]{:S(2)}, u32[]{:S(2)}) async-start(bf16[24,48,128]{2,1,0:T(8,128)(2,1)} %get-tuple-element.52), calls=%async_computation | async-start | bytes 589824 | tf_op jit(solution)/shard_map/all_to_all | solution.py:244
  89.4 23.3 %collective-permute-start.11 = (bf16[512,512]{1,0:T(8,128)(2,1)}, bf16[512,512]{1,0:T(8,128)(2,1)}, u32[]{:S(2)}, u32[]{:S(2)}) collective-permute-start(bf16[512,512]{1,0:T(8,128)(2,1)} %get-tuple-element.46), channel_id=1, source_target_pairs={{0,4},{1,29},{2,6},{3,31},{4,8},{5,1},{6,10},{7,3},{8,12},{9,5},{1... | collective-permute-start | bytes 1572872 | tf_op jit(solution)/shard_map/ppermute | solution.py:38
  91.3 21.4 %collective-permute-start.12 = (bf16[512,512]{1,0:T(8,128)(2,1)}, bf16[512,512]{1,0:T(8,128)(2,1)}, u32[]{:S(2)}, u32[]{:S(2)}) collective-permute-start(bf16[512,512]{1,0:T(8,128)(2,1)} %get-tuple-element.47), channel_id=1, source_target_pairs={{0,28},{1,5},{2,30},{3,7},{4,0},{5,9},{6,2},{7,11},{8,4},{9,13},{1... | collective-permute-start | bytes 1572872 | tf_op jit(solution)/shard_map/ppermute | solution.py:38
  103.3 23.7 %all-to-all-start.1 = ((bf16[24,48,128]{2,1,0:T(8,128)(2,1)}), bf16[24,48,128]{2,1,0:T(8,128)(2,1)S(1)}, u32[]{:S(2)}, u32[]{:S(2)}) async-start(bf16[24,48,128]{2,1,0:T(8,128)(2,1)} %shard_map.128), calls=%async_computation.1 | async-start | bytes 589824 | tf_op jit(solution)/shard_map/all_to_all | solution.py:248
  110.8 8.3 %collective-permute-start.10 = (bf16[256,512]{1,0:T(8,128)(2,1)S(1)}, bf16[256,512]{1,0:T(8,128)(2,1)S(1)}, u32[]{:S(2)}, u32[]{:S(2)}) collective-permute-start(bf16[256,512]{1,0:T(8,128)(2,1)S(1)} %collective-permute-done.9.w6), channel_id=1, source_target_pairs={{0,8},{1,25},{2,10},{3,27},{4,12},{5,29},{6,14},{7,31},{8,16},{9,1... | collective-permute-start | bytes 786440 | tf_op jit(solution)/shard_map/ppermute | solution.py:38
  119.3 7.0 %collective-permute-start.13 = (bf16[192,512]{1,0:T(8,128)(2,1)S(1)}, bf16[192,512]{1,0:T(8,128)(2,1)S(1)}, u32[]{:S(2)}, u32[]{:S(2)}) collective-permute-start(bf16[192,512]{1,0:T(8,128)(2,1)S(1)} %get-tuple-element.51), channel_id=1, source_target_pairs={{0,1},{1,0},{2,3},{3,2},{4,5},{5,4},{6,7},{7,6},{8,9},{9,8},{10,11... | collective-permute-start | bytes 589832 | tf_op jit(solution)/shard_map/ppermute | solution.py:38

commit v4 on v3

--- a/solution.py
+++ b/solution.py
@@ -233,7 +233,8 @@
     (far,) = call(far_kernel, (piece(128),), [VMEM] * 5, d0, a, b, e2, e6)
     far = send(far, ZSWAP)
     w6, w2 = send(w0, ring(2)), send(w0, ring(-2))
-    w2, far, w6 = lax.optimization_barrier((w2, far, w6))
+    left, right = call(join_kernel, (piece(512), piece(512)), [VMEM] * 3, w0, w2, w6)
+    left, far, right, w6 = lax.optimization_barrier((left, far, right, w6))
     shard = (weights.shape, F32)
     block = -(-64 // replicas) * 16
     first_new, second_new, blocks = call(
@@ -242,9 +243,9 @@
     )
     blocks, w0 = lax.optimization_barrier((blocks, w0))
     got = lax.all_to_all(blocks, "rep", split_axis=0, concat_axis=0, tiled=True)
-    left, right = call(join_kernel, (piece(512), piece(512)), [VMEM] * 3, w0, w2, w6)
     from_left, from_right, w4 = send(left, ring(1)), send(right, ring(-1)), send(w6, ring(2))
     (mean,) = call(mean_kernel, ((got.shape, BF16),), [SMEM, VMEM], partner, got)
+    w4, mean = lax.optimization_barrier((w4, mean))
     back = lax.all_to_all(mean, "rep", split_axis=0, concat_axis=0, tiled=True)
     partial = ((tokens, 512), F32)
     mine, theirs = call(

time: 129 us -> 128 us (level)
  the two profiles are of different devices: /device:TPU:43 before, /device:TPU:1 now
where the time goes in v4:
time: 128 us; the launch traced here: 127 us
  starting transfers between devices  90.6 us (71%)
  waiting for transfers between devices  23.8 us (19%)
  Pallas kernels  9.96 us (8%)
    ppermute x14, starting transfers between devices, send(): return lax.ppermute(value, 'fsdp', pairs)  70.2 us
    ppermute x14, waiting for transfers between devices, send(): return lax.ppermute(value, 'fsdp', pairs)  15.3 us
    all_to_all x1, starting transfers between devices, on_device(): got = lax.all_to_all(blocks, 'rep', split_axis=0, concat_axis=0, tiled=True)  10.3 us
    all_to_all x1, starting transfers between devices, on_device(): back = lax.all_to_all(mean, 'rep', split_axis=0, concat_axis=0, tiled=True)  10 us
    all_to_all x1, waiting for transfers between devices, on_device(): back = lax.all_to_all(mean, 'rep', split_axis=0, concat_axis=0, tiled=True)  8.51 us
    pallas_call x9, Pallas kernels, call(): pl.pallas_call(kernel, out_shape=tuple((jax.ShapeDtypeStruct(shape, kind)...  7.28 us
    pallas_call x2, Pallas kernels, pick(): pl.pallas_call(lambda *refs: pick_kernel(away, *refs), out_shape=jax.Shap...  2.68 us
  transfers between devices with their start and end apart: 16, of which 7 were waited for; matrix products, arithmetic and copies ran while one was open for 1% of the time, Pallas kernels for 4%

profile of v4, /device:TPU:1, one launch (start us, length us, event | category | flops | bytes accessed | tf_op | source)
XLA Modules:
  0.0 126.9 jit_solution(16898584090898956042)
XLA Ops:
  0.6 1.4 %shard_map.120 = bf16[192,2560]{1,0:T(8,128)(2,1)S(1)} custom-call(bf16[192,4096]{1,0:T(8,128)(2,1)} %refs_0_.3, bf16[192,512]{1,0:T(8,128)(2,1)} %refs_2_.1), custom_call_target="tpu_custom_call" | custom-call | tf_op jit(solution)/shard_map/pallas_call | solution.py:74
  2.0 12.6 %collective-permute-start = (bf16[192,2560]{1,0:T(8,128)(2,1)S(1)}, bf16[192,2560]{1,0:T(8,128)(2,1)S(1)}, u32[]{:S(2)}, u32[]{:S(2)}) collective-permute-start(bf16[192,2560]{1,0:T(8,128)(2,1)S(1)} %shard_map.120), channel_id=1, source_target_pairs={{0,1},{1,0},{2,3},{3,2},{4,5},{5,4},{6,7},{7,6},{8,9},{9,8},{10,11... | collective-permute-start | bytes 2949128 | tf_op jit(solution)/shard_map/ppermute | solution.py:38
  14.6 1.3 %shard_map.119.refs_0_.own = bf16[192,2048]{1,0:T(8,128)(2,1)S(1)} custom-call(bf16[192,4096]{1,0:T(8,128)(2,1)} %refs_0_.3), custom_call_target="tpu_custom_call" | custom-call | tf_op jit(solution)/shard_map/pallas_call | solution.py:74
  15.9 0.8 collective-permute-done.refs_1_.other
  16.8 1.3 %shard_map.122 = (bf16[512,512]{1,0:T(8,128)(2,1)S(1)}, bf16[512,512]{1,0:T(8,128)(2,1)S(1)}, bf16[256,512]{1,0:T(8,128)(2,1)S(1)}, f32[256,512]{1,0:T(8,128)S(1...) custom-call(bf16[192,2048]{1,0:T(8,128)(2,1)S(1)} %shard_map.119.refs_0_.own, ...), custom_call_target="tpu_custom_call" | custom-call | flops 805306368 | bytes 1048576 | tf_op jit(solution)/shard_map/pallas_call | solution.py:85
  18.0 1.9 %collective-permute-start.4 = (bf16[512,512]{1,0:T(8,128)(2,1)S(1)}, bf16[512,512]{1,0:T(8,128)(2,1)S(1)}, u32[]{:S(2)}, u32[]{:S(2)}) collective-permute-start(bf16[512,512]{1,0:T(8,128)(2,1)S(1)} %get-tuple-element.38), channel_id=1, source_target_pairs={{0,4},{1,29},{2,6},{3,31},{4,8},{5,1},{6,10},{7,3},{8,12},{9,5},{1... | collective-permute-start | bytes 1572872 | tf_op jit(solution)/shard_map/ppermute | solution.py:38
  20.0 3.4 %collective-permute-start.5 = (bf16[512,512]{1,0:T(8,128)(2,1)S(1)}, bf16[512,512]{1,0:T(8,128)(2,1)S(1)}, u32[]{:S(2)}, u32[]{:S(2)}) collective-permute-start(bf16[512,512]{1,0:T(8,128)(2,1)S(1)} %get-tuple-element.39), channel_id=1, source_target_pairs={{0,28},{1,5},{2,30},{3,7},{4,0},{5,9},{6,2},{7,11},{8,4},{9,13},{1... | collective-permute-start | bytes 1572872 | tf_op jit(solution)/shard_map/ppermute | solution.py:38
  23.3 1.9 %collective-permute-start.6 = (bf16[256,512]{1,0:T(8,128)(2,1)S(1)}, bf16[256,512]{1,0:T(8,128)(2,1)S(1)}, u32[]{:S(2)}, u32[]{:S(2)}) collective-permute-start(bf16[256,512]{1,0:T(8,128)(2,1)S(1)} %get-tuple-element.42), channel_id=1, source_target_pairs={{0,8},{1,25},{2,10},{3,27},{4,12},{5,29},{6,14},{7,31},{8,16},{9,1... | collective-permute-start | bytes 786440 | tf_op jit(solution)/shard_map/ppermute | solution.py:38
  25.3 9.8 %collective-permute-start.1 = (bf16[128,512]{1,0:T(8,128)(2,1)S(1)}, bf16[128,512]{1,0:T(8,128)(2,1)S(1)}, u32[]{:S(2)}, u32[]{:S(2)}) collective-permute-start(bf16[128,512]{1,0:T(8,128)(2,1)S(1)} %convert_bitcast_fusion), channel_id=1, source_target_pairs={{0,2},{1,3},{2,0},{3,1},{4,6},{5,7},{6,4},{7,5},{8,10},{9,11},{10,... | collective-permute-start | bytes 393224 | tf_op jit(solution)/shard_map/ppermute | solution.py:38
  35.1 4.7 %collective-permute-done.5.b = bf16[512,512]{1,0:T(8,128)(2,1)S(1)} collective-permute-done((bf16[512,512]{1,0:T(8,128)(2,1)S(1)}, bf16[512,512]{1,0:T(8,128)(2,1)S(1)}, u32[]{:S(2)}, u32[]{:S(2)}) %collective-permute-start.5) | collective-permute-done | bytes 524320 | tf_op jit(solution)/shard_map/ppermute | solution.py:38
  40.0 1.9 %collective-permute-start.7 = (bf16[256,512]{1,0:T(8,128)(2,1)S(1)}, bf16[256,512]{1,0:T(8,128)(2,1)S(1)}, u32[]{:S(2)}, u32[]{:S(2)}) collective-permute-start(bf16[256,512]{1,0:T(8,128)(2,1)S(1)} %get-tuple-element.43), channel_id=1, source_target_pairs={{0,8},{1,25},{2,10},{3,27},{4,12},{5,29},{6,14},{7,31},{8,16},{9,1... | collective-permute-start | bytes 786440 | tf_op jit(solution)/shard_map/ppermute | solution.py:38
  41.9 4.3 %collective-permute-start.8 = (bf16[256,512]{1,0:T(8,128)(2,1)S(1)}, bf16[256,512]{1,0:T(8,128)(2,1)S(1)}, u32[]{:S(2)}, u32[]{:S(2)}) collective-permute-start(bf16[256,512]{1,0:T(8,128)(2,1)S(1)} %get-tuple-element.44), channel_id=1, source_target_pairs={{0,24},{1,9},{2,26},{3,11},{4,28},{5,13},{6,30},{7,15},{8,0},{9,17... | collective-permute-start | bytes 786440 | tf_op jit(solution)/shard_map/ppermute | solution.py:38
  46.3 2.1 %collective-permute-start.2 = (bf16[256,512]{1,0:T(8,128)(2,1)S(1)}, bf16[256,512]{1,0:T(8,128)(2,1)S(1)}, u32[]{:S(2)}, u32[]{:S(2)}) collective-permute-start(bf16[256,512]{1,0:T(8,128)(2,1)S(1)} %constant_dynamic-update-slice_fusion.w0), channel_id=1, source_target_pairs={{0,24},{1,9},{2,26},{3,11},{4,28},{5,13},{6,30},{7,15},{8,0},{9,17... | collective-permute-start | bytes 786440 | tf_op jit(solution)/shard_map/ppermute | solution.py:38
  48.3 5.5 %collective-permute-start.3 = (bf16[256,512]{1,0:T(8,128)(2,1)S(1)}, bf16[256,512]{1,0:T(8,128)(2,1)S(1)}, u32[]{:S(2)}, u32[]{:S(2)}) collective-permute-start(bf16[256,512]{1,0:T(8,128)(2,1)S(1)} %constant_dynamic-update-slice_fusion.w0), channel_id=1, source_target_pairs={{0,8},{1,25},{2,10},{3,27},{4,12},{5,29},{6,14},{7,31},{8,16},{9,1... | collective-permute-start | bytes 786440 | tf_op jit(solution)/shard_map/ppermute | solution.py:38
  53.8 1.6 %collective-permute-done.7.e2 = bf16[256,512]{1,0:T(8,128)(2,1)S(1)} collective-permute-done((bf16[256,512]{1,0:T(8,128)(2,1)S(1)}, bf16[256,512]{1,0:T(8,128)(2,1)S(1)}, u32[]{:S(2)}, u32[]{:S(2)}) %collective-permute-start.7) | collective-permute-done | bytes 262176 | tf_op jit(solution)/shard_map/ppermute | solution.py:38
  55.4 1.5 %collective-permute-done.8.e6 = bf16[256,512]{1,0:T(8,128)(2,1)S(1)} collective-permute-done((bf16[256,512]{1,0:T(8,128)(2,1)S(1)}, bf16[256,512]{1,0:T(8,128)(2,1)S(1)}, u32[]{:S(2)}, u32[]{:S(2)}) %collective-permute-start.8) | collective-permute-done | bytes 262176 | tf_op jit(solution)/shard_map/ppermute | solution.py:38
  57.0 7.4 %collective-permute-start.9 = (bf16[128,512]{1,0:T(8,128)(2,1)S(1)}, bf16[128,512]{1,0:T(8,128)(2,1)S(1)}, u32[]{:S(2)}, u32[]{:S(2)}) collective-permute-start(bf16[128,512]{1,0:T(8,128)(2,1)S(1)} %shard_map.124), channel_id=1, source_target_pairs={{0,2},{1,3},{2,0},{3,1},{4,6},{5,7},{6,4},{7,5},{8,10},{9,11},{10,... | collective-permute-start | bytes 393224 | tf_op jit(solution)/shard_map/ppermute | solution.py:38
  64.4 5.2 %collective-permute-done.2.w2 = bf16[256,512]{1,0:T(8,128)(2,1)S(1)} collective-permute-done((bf16[256,512]{1,0:T(8,128)(2,1)S(1)}, bf16[256,512]{1,0:T(8,128)(2,1)S(1)}, u32[]{:S(2)}, u32[]{:S(2)}) %collective-permute-start.2) | collective-permute-done | bytes 262176 | tf_op jit(solution)/shard_map/ppermute | solution.py:38
  69.7 0.8 copy-done.8
  70.5 1.2 shard_map.125
  71.7 10.3 %all-to-all-start = ((bf16[24,48,128]{2,1,0:T(8,128)(2,1)}), bf16[24,48,128]{2,1,0:T(8,128)(2,1)S(1)}, u32[]{:S(2)}, u32[]{:S(2)}) async-start(bf16[24,48,128]{2,1,0:T(8,128)(2,1)} %get-tuple-element.49), calls=%async_computation | async-start | bytes 589824 | tf_op jit(solution)/shard_map/all_to_all | solution.py:245
  82.1 1.9 %collective-permute-start.10 = (bf16[256,512]{1,0:T(8,128)(2,1)S(1)}, bf16[256,512]{1,0:T(8,128)(2,1)S(1)}, u32[]{:S(2)}, u32[]{:S(2)}) collective-permute-start(bf16[256,512]{1,0:T(8,128)(2,1)S(1)} %collective-permute-done.3.w6), channel_id=1, source_target_pairs={{0,8},{1,25},{2,10},{3,27},{4,12},{5,29},{6,14},{7,31},{8,16},{9,1... | collective-permute-start | bytes 786440 | tf_op jit(solution)/shard_map/ppermute | solution.py:38
  84.0 13.8 %collective-permute-start.11 = (bf16[512,512]{1,0:T(8,128)(2,1)}, bf16[512,512]{1,0:T(8,128)(2,1)}, u32[]{:S(2)}, u32[]{:S(2)}) collective-permute-start(bf16[512,512]{1,0:T(8,128)(2,1)} %copy-done.8), channel_id=1, source_target_pairs={{0,4},{1,29},{2,6},{3,31},{4,8},{5,1},{6,10},{7,3},{8,12},{9,5},{1... | collective-permute-start | bytes 1572872 | tf_op jit(solution)/shard_map/ppermute | solution.py:38
  97.8 1.9 %collective-permute-start.12 = (bf16[512,512]{1,0:T(8,128)(2,1)}, bf16[512,512]{1,0:T(8,128)(2,1)}, u32[]{:S(2)}, u32[]{:S(2)}) collective-permute-start(bf16[512,512]{1,0:T(8,128)(2,1)} %copy-done.7), channel_id=1, source_target_pairs={{0,28},{1,5},{2,30},{3,7},{4,0},{5,9},{6,2},{7,11},{8,4},{9,13},{1... | collective-permute-start | bytes 1572872 | tf_op jit(solution)/shard_map/ppermute | solution.py:38
  99.7 1.3 %shard_map.126 = bf16[24,48,128]{2,1,0:T(8,128)(2,1)} custom-call(s32[1,24]{1,0:T(1,128)S(1)} %copy-done.6, bf16[24,48,128]{2,1,0:T(8,128)(2,1)S(1)} %all-to-all-done.got), custom_call_target="tpu_custom_call" | custom-call | bytes 1048576 | tf_op jit(solution)/shard_map/pallas_call | solution.py:85
  101.1 10.0 %all-to-all-start.1 = ((bf16[24,48,128]{2,1,0:T(8,128)(2,1)}), bf16[24,48,128]{2,1,0:T(8,128)(2,1)S(1)}, u32[]{:S(2)}, u32[]{:S(2)}) async-start(bf16[24,48,128]{2,1,0:T(8,128)(2,1)} %shard_map.126), calls=%async_computation.1 | async-start | bytes 589824 | tf_op jit(solution)/shard_map/all_to_all | solution.py:249
  111.1 2.1 %shard_map.127 = (f32[192,512]{1,0:T(8,128)S(1)}, f32[192,512]{1,0:T(8,128)S(1)}) custom-call(bf16[192,2048]{1,0:T(8,128)(2,1)S(1)} %shard_map.119.refs_0_.own, bf16[192,2560]{1,0:T(8,128)(2,1)S(1)} %collective-permute-done.refs_1_.other, bf16[256,512]{1,0:T(8,128)(2,1)S(1)} %constant_dynamic-update-slice_fusion.w0, ...), custom_call_target="tpu_custom_call" | custom-call | flops 805306368 | bytes 1048576 | tf_op jit(solution)/shard_map/pallas_call | solution.py:85
  113.5 1.9 %collective-permute-start.13 = (bf16[192,512]{1,0:T(8,128)(2,1)S(1)}, bf16[192,512]{1,0:T(8,128)(2,1)S(1)}, u32[]{:S(2)}, u32[]{:S(2)}) collective-permute-start(bf16[192,512]{1,0:T(8,128)(2,1)S(1)} %get-tuple-element.57), channel_id=1, source_target_pairs={{0,1},{1,0},{2,3},{3,2},{4,5},{5,4},{6,7},{7,6},{8,9},{9,8},{10,11... | collective-permute-start | bytes 589832 | tf_op jit(solution)/shard_map/ppermute | solution.py:38
  115.4 1.4 %collective-permute-done.13 = bf16[192,512]{1,0:T(8,128)(2,1)S(1)} collective-permute-done((bf16[192,512]{1,0:T(8,128)(2,1)S(1)}, bf16[192,512]{1,0:T(8,128)(2,1)S(1)}, u32[]{:S(2)}, u32[]{:S(2)}) %collective-permute-start.13) | collective-permute-done | bytes 196640 | tf_op jit(solution)/shard_map/ppermute | solution.py:38
  116.8 0.7 add_convert_fusion
  117.5 8.5 %all-to-all-done.1.back = bf16[24,48,128]{2,1,0:T(8,128)(2,1)S(1)} async-done(((bf16[24,48,128]{2,1,0:T(8,128)(2,1)}), bf16[24,48,128]{2,1,0:T(8,128)(2,1)S(1)}, u32[]{:S(2)}, u32[]{:S(2)}) %all-to-all-start.1) | async-done | bytes 294944 | tf_op jit(solution)/shard_map/all_to_all | solution.py:249
  126.1 0.9 shard_map.129
  (33 shorter events, 0.7 us)
Async XLA Ops:
  2.0 13.9 %copy-start = (f32[1,128,512]{2,1,0:T(8,128)S(1)}, f32[1,128,512]{2,1,0:T(8,128)}, u32[]{:S(2)}) copy-start(f32[1,128,512]{2,1,0:T(8,128)} %weight.1) | copy-start | bytes 786436
  2.0 14.8 %copy-start.5 = (bf16[192,512]{1,0:T(8,128)(2,1)S(1)}, bf16[192,512]{1,0:T(8,128)(2,1)}, u32[]{:S(2)}) copy-start(bf16[192,512]{1,0:T(8,128)(2,1)} %refs_2_.1) | copy-start | bytes 589828
  2.0 14.7 %collective-permute-start = (bf16[192,2560]{1,0:T(8,128)(2,1)S(1)}, bf16[192,2560]{1,0:T(8,128)(2,1)S(1)}, u32[]{:S(2)}, u32[]{:S(2)}) collective-permute-start(bf16[192,2560]{1,0:T(8,128)(2,1)S(1)} %shard_map.120), channel_id=1, source_target_pairs={{0,1},{1,0},{2,3},{3,2},{4,5},{5,4},{6,7},{7,6},{8,9},{9,8},{10,11... | collective-permute-start | bytes 2949128 | tf_op jit(solution)/shard_map/ppermute | solution.py:38
  18.0 17.1 %collective-permute-start.4 = (bf16[512,512]{1,0:T(8,128)(2,1)S(1)}, bf16[512,512]{1,0:T(8,128)(2,1)S(1)}, u32[]{:S(2)}, u32[]{:S(2)}) collective-permute-start(bf16[512,512]{1,0:T(8,128)(2,1)S(1)} %get-tuple-element.38), channel_id=1, source_target_pairs={{0,4},{1,29},{2,6},{3,31},{4,8},{5,1},{6,10},{7,3},{8,12},{9,5},{1... | collective-permute-start | bytes 1572872 | tf_op jit(solution)/shard_map/ppermute | solution.py:38
  20.0 19.9 %collective-permute-start.5 = (bf16[512,512]{1,0:T(8,128)(2,1)S(1)}, bf16[512,512]{1,0:T(8,128)(2,1)S(1)}, u32[]{:S(2)}, u32[]{:S(2)}) collective-permute-start(bf16[512,512]{1,0:T(8,128)(2,1)S(1)} %get-tuple-element.39), channel_id=1, source_target_pairs={{0,28},{1,5},{2,30},{3,7},{4,0},{5,9},{6,2},{7,11},{8,4},{9,13},{1... | collective-permute-start | bytes 1572872 | tf_op jit(solution)/shard_map/ppermute | solution.py:38
  23.3 11.7 %collective-permute-start.6 = (bf16[256,512]{1,0:T(8,128)(2,1)S(1)}, bf16[256,512]{1,0:T(8,128)(2,1)S(1)}, u32[]{:S(2)}, u32[]{:S(2)}) collective-permute-start(bf16[256,512]{1,0:T(8,128)(2,1)S(1)} %get-tuple-element.42), channel_id=1, source_target_pairs={{0,8},{1,25},{2,10},{3,27},{4,12},{5,29},{6,14},{7,31},{8,16},{9,1... | collective-permute-start | bytes 786440 | tf_op jit(solution)/shard_map/ppermute | solution.py:38
  25.3 20.9 %collective-permute-start.1 = (bf16[128,512]{1,0:T(8,128)(2,1)S(1)}, bf16[128,512]{1,0:T(8,128)(2,1)S(1)}, u32[]{:S(2)}, u32[]{:S(2)}) collective-permute-start(bf16[128,512]{1,0:T(8,128)(2,1)S(1)} %convert_bitcast_fusion), channel_id=1, source_target_pairs={{0,2},{1,3},{2,0},{3,1},{4,6},{5,7},{6,4},{7,5},{8,10},{9,11},{10,... | collective-permute-start | bytes 393224 | tf_op jit(solution)/shard_map/ppermute | solution.py:38
  40.0 15.5 %collective-permute-start.7 = (bf16[256,512]{1,0:T(8,128)(2,1)S(1)}, bf16[256,512]{1,0:T(8,128)(2,1)S(1)}, u32[]{:S(2)}, u32[]{:S(2)}) collective-permute-start(bf16[256,512]{1,0:T(8,128)(2,1)S(1)} %get-tuple-element.43), channel_id=1, source_target_pairs={{0,8},{1,25},{2,10},{3,27},{4,12},{5,29},{6,14},{7,31},{8,16},{9,1... | collective-permute-start | bytes 786440 | tf_op jit(solution)/shard_map/ppermute | solution.py:38
  41.9 15.1 %collective-permute-start.8 = (bf16[256,512]{1,0:T(8,128)(2,1)S(1)}, bf16[256,512]{1,0:T(8,128)(2,1)S(1)}, u32[]{:S(2)}, u32[]{:S(2)}) collective-permute-start(bf16[256,512]{1,0:T(8,128)(2,1)S(1)} %get-tuple-element.44), channel_id=1, source_target_pairs={{0,24},{1,9},{2,26},{3,11},{4,28},{5,13},{6,30},{7,15},{8,0},{9,17... | collective-permute-start | bytes 786440 | tf_op jit(solution)/shard_map/ppermute | solution.py:38
  46.2 24.3 %copy-start.1 = (f32[1,128,512]{2,1,0:T(8,128)S(1)}, f32[1,128,512]{2,1,0:T(8,128)}, u32[]{:S(2)}) copy-start(f32[1,128,512]{2,1,0:T(8,128)} %anchor.3) | copy-start | bytes 786436
  46.2 24.3 %copy-start.2 = (f32[1,128,512]{2,1,0:T(8,128)S(1)}, f32[1,128,512]{2,1,0:T(8,128)}, u32[]{:S(2)}) copy-start(f32[1,128,512]{2,1,0:T(8,128)} %first.1) | copy-start | bytes 786436
  46.2 24.3 %copy-start.3 = (f32[1,128,512]{2,1,0:T(8,128)S(1)}, f32[1,128,512]{2,1,0:T(8,128)}, u32[]{:S(2)}) copy-start(f32[1,128,512]{2,1,0:T(8,128)} %second.1) | copy-start | bytes 786436
  46.2 24.3 %copy-start.4 = (f32[1,128,512]{2,1,0:T(8,128)S(1)}, f32[1,128,512]{2,1,0:T(8,128)}, u32[]{:S(2)}) copy-start(f32[1,128,512]{2,1,0:T(8,128)} %mom.1) | copy-start | bytes 786436
  46.3 23.4 %collective-permute-start.2 = (bf16[256,512]{1,0:T(8,128)(2,1)S(1)}, bf16[256,512]{1,0:T(8,128)(2,1)S(1)}, u32[]{:S(2)}, u32[]{:S(2)}) collective-permute-start(bf16[256,512]{1,0:T(8,128)(2,1)S(1)} %constant_dynamic-update-slice_fusion.w0), channel_id=1, source_target_pairs={{0,24},{1,9},{2,26},{3,11},{4,28},{5,13},{6,30},{7,15},{8,0},{9,17... | collective-permute-start | bytes 786440 | tf_op jit(solution)/shard_map/ppermute | solution.py:38
  48.3 21.3 %collective-permute-start.3 = (bf16[256,512]{1,0:T(8,128)(2,1)S(1)}, bf16[256,512]{1,0:T(8,128)(2,1)S(1)}, u32[]{:S(2)}, u32[]{:S(2)}) collective-permute-start(bf16[256,512]{1,0:T(8,128)(2,1)S(1)} %constant_dynamic-update-slice_fusion.w0), channel_id=1, source_target_pairs={{0,8},{1,25},{2,10},{3,27},{4,12},{5,29},{6,14},{7,31},{8,16},{9,1... | collective-permute-start | bytes 786440 | tf_op jit(solution)/shard_map/ppermute | solution.py:38
  57.0 13.5 %collective-permute-start.9 = (bf16[128,512]{1,0:T(8,128)(2,1)S(1)}, bf16[128,512]{1,0:T(8,128)(2,1)S(1)}, u32[]{:S(2)}, u32[]{:S(2)}) collective-permute-start(bf16[128,512]{1,0:T(8,128)(2,1)S(1)} %shard_map.124), channel_id=1, source_target_pairs={{0,2},{1,3},{2,0},{3,1},{4,6},{5,7},{6,4},{7,5},{8,10},{9,11},{10,... | collective-permute-start | bytes 393224 | tf_op jit(solution)/shard_map/ppermute | solution.py:38
  69.7 0.8 copy-start.8
  70.5 1.2 copy-start.7
  70.5 29.2 %copy-start.6 = (s32[1,24]{1,0:T(1,128)S(1)}, s32[1,24]{1,0:T(1,128)}, u32[]{:S(2)}) copy-start(s32[1,24]{1,0:T(1,128)} %matching.1) | copy-start | bytes 292
  71.7 28.0 %all-to-all-start = ((bf16[24,48,128]{2,1,0:T(8,128)(2,1)}), bf16[24,48,128]{2,1,0:T(8,128)(2,1)S(1)}, u32[]{:S(2)}, u32[]{:S(2)}) async-start(bf16[24,48,128]{2,1,0:T(8,128)(2,1)} %get-tuple-element.49), calls=%async_computation | async-start | bytes 589824 | tf_op jit(solution)/shard_map/all_to_all | solution.py:245
  82.1 19.0 %collective-permute-start.10 = (bf16[256,512]{1,0:T(8,128)(2,1)S(1)}, bf16[256,512]{1,0:T(8,128)(2,1)S(1)}, u32[]{:S(2)}, u32[]{:S(2)}) collective-permute-start(bf16[256,512]{1,0:T(8,128)(2,1)S(1)} %collective-permute-done.3.w6), channel_id=1, source_target_pairs={{0,8},{1,25},{2,10},{3,27},{4,12},{5,29},{6,14},{7,31},{8,16},{9,1... | collective-permute-start | bytes 786440 | tf_op jit(solution)/shard_map/ppermute | solution.py:38
  84.0 27.1 %collective-permute-start.11 = (bf16[512,512]{1,0:T(8,128)(2,1)}, bf16[512,512]{1,0:T(8,128)(2,1)}, u32[]{:S(2)}, u32[]{:S(2)}) collective-permute-start(bf16[512,512]{1,0:T(8,128)(2,1)} %copy-done.8), channel_id=1, source_target_pairs={{0,4},{1,29},{2,6},{3,31},{4,8},{5,1},{6,10},{7,3},{8,12},{9,5},{1... | collective-permute-start | bytes 1572872 | tf_op jit(solution)/shard_map/ppermute | solution.py:38
  97.8 13.3 %collective-permute-start.12 = (bf16[512,512]{1,0:T(8,128)(2,1)}, bf16[512,512]{1,0:T(8,128)(2,1)}, u32[]{:S(2)}, u32[]{:S(2)}) collective-permute-start(bf16[512,512]{1,0:T(8,128)(2,1)} %copy-done.7), channel_id=1, source_target_pairs={{0,28},{1,5},{2,30},{3,7},{4,0},{5,9},{6,2},{7,11},{8,4},{9,13},{1... | collective-permute-start | bytes 1572872 | tf_op jit(solution)/shard_map/ppermute | solution.py:38
  101.1 25.0 %all-to-all-start.1 = ((bf16[24,48,128]{2,1,0:T(8,128)(2,1)}), bf16[24,48,128]{2,1,0:T(8,128)(2,1)S(1)}, u32[]{:S(2)}, u32[]{:S(2)}) async-start(bf16[24,48,128]{2,1,0:T(8,128)(2,1)} %shard_map.126), calls=%async_computation.1 | async-start | bytes 589824 | tf_op jit(solution)/shard_map/all_to_all | solution.py:249
  113.5 3.3 %collective-permute-start.13 = (bf16[192,512]{1,0:T(8,128)(2,1)S(1)}, bf16[192,512]{1,0:T(8,128)(2,1)S(1)}, u32[]{:S(2)}, u32[]{:S(2)}) collective-permute-start(bf16[192,512]{1,0:T(8,128)(2,1)S(1)} %get-tuple-element.57), channel_id=1, source_target_pairs={{0,1},{1,0},{2,3},{3,2},{4,5},{5,4},{6,7},{7,6},{8,9},{9,8},{10,11... | collective-permute-start | bytes 589832 | tf_op jit(solution)/shard_map/ppermute | solution.py:38
